TPU v7x, 256 devices: a whole 4x4x8 slice. The times are simulated.
256 devices in a mesh: group: 64 (over z, x, core), head: 4 (over y).
Axes of the slice: x: 4, y: 4, z: 8, core: 2. Of those that a mesh axis runs over, the one named last changes fastest.
Arguments:
- hidden: bfloat16 [16384, 3072], P(('group', 'head')), may hold values from -4 to 4
- query: bfloat16 [16384, 1536], P(('group', 'head')), may hold values from -128 to 128
- keys: bfloat16 [16384, 1536], P(('group', 'head')), may hold values from -4 to 4
- values: bfloat16 [16384, 1536], P(('group', 'head')), may hold values from -6 to 6
- attends: int32 [64, 64], P('group'), may hold values from 0 to 1, as said below
- levels: int32 [64], P('group'), may hold values from 0 to 63
- out_weight: bfloat16 [1536, 3072], P('head'), may hold values from -1.25 to 1.25
- gate_table: float32 [64, 3072], replicated, may hold values from -6 to 6
Outputs:
- updated: bfloat16 [16384, 3072], P(('group', 'head'))
Inputs may be any that keep to these rules, and one draw needn't show every extreme that they name: attends[c, c] is 1 and attends[c, j] is 0 for j > c; how many earlier groups a group attends to differs from group to group.
All inputs are finite; a program needn't handle non-finite values.
Results may differ from a plain program's by a relative error of at most 0.017.
Values may be sent and summed in bfloat16 or wider, within the bound.
A program may use at most 192 MiB of HBM per device.

v0:
```python
import jax
import jax.numpy as jnp
from jax import lax
from jax.sharding import PartitionSpec as P

HS = 128


def from_behind(block, axis, distance):
    devices = range(lax.axis_size(axis))
    route = [(i - distance, i) for i in devices if i - distance in devices]
    return lax.ppermute(block, axis, route)


def shards(hidden, query, keys, values, attends, levels, out_weight, gate_table):
    local_query, local_keys, local_values = (
        lax.all_to_all(query, "head", split_axis=1, concat_axis=0, tiled=True),
        lax.all_to_all(keys, "head", split_axis=1, concat_axis=0, tiled=True),
        lax.all_to_all(values, "head", split_axis=1, concat_axis=0, tiled=True),
    )
    row_count = local_query.shape[0]
    width_here = local_query.shape[1]
    heads_here = width_here // HS
    query_three = local_query.reshape(row_count, heads_here, HS)
    score_scale = HS ** (-0.5)
    attend_row = attends[0]
    group_count = attend_row.shape[0]
    group_id = lax.axis_index("group")
    initial = (
        jnp.full((heads_here, row_count), -1e30, jnp.float32),
        jnp.zeros((heads_here, row_count), jnp.float32),
        jnp.zeros((heads_here, row_count, HS), jnp.float32),
    )

    def absorb(softmax_state, key_block, value_block, allowed):
        running_top, running_total, running_sum = softmax_state
        block_rows = key_block.shape[0]
        key_three = key_block.reshape(block_rows, heads_here, HS)
        value_three = value_block.reshape(block_rows, heads_here, HS)
        scores = (
            jnp.einsum("qhd,khd->hqk", query_three, key_three, preferred_element_type=jnp.float32)
            * score_scale
        )
        scores = jnp.where(allowed[None, None, :], scores, -1e30)
        new_top = jnp.maximum(running_top, jnp.max(scores, axis=-1))
        weights = jnp.where(allowed[None, None, :], jnp.exp(scores - new_top[:, :, None]), 0.0)
        factor = jnp.exp(running_top - new_top)
        running_total = running_total * factor + jnp.sum(weights, axis=-1)
        running_sum = running_sum * factor[:, :, None] + jnp.einsum(
            "hqk,khd->hqd",
            weights.astype(jnp.bfloat16),
            value_three,
            preferred_element_type=jnp.float32,
        )
        return (new_top, running_total, running_sum)

    def consider(softmax_state, key_block, value_block, allowed):
        return absorb(softmax_state, key_block, value_block, allowed)

    own_allowed = jnp.ones((row_count,), jnp.bool_)
    first_state = absorb(initial, local_keys, local_values, own_allowed)

    def chain_step(step_index, carried):
        moving, softmax_state = carried
        moving = from_behind((moving[0], moving[1]), "group", 1)
        source = group_id - step_index
        clipped = jnp.clip(source, 0, group_count - 1)
        listed = (source >= 0) & (
            lax.dynamic_index_in_dim(attend_row, clipped, 0, keepdims=False) > 0
        )
        allowed = jnp.full((row_count,), listed)
        softmax_state = consider(softmax_state, moving[0], moving[1], allowed)
        return (moving, softmax_state)

    final_pair = lax.fori_loop(
        1, lax.axis_size("group"), chain_step, ((local_keys, local_values), first_state)
    )
    final_state = final_pair[1]
    running_top, running_total, running_sum = final_state
    attended = running_sum / running_total[:, :, None]
    attended = (
        jnp.transpose(attended, (1, 0, 2)).reshape(row_count, width_here).astype(jnp.bfloat16)
    )
    projected = lax.psum_scatter(
        jnp.dot(attended, out_weight, preferred_element_type=jnp.float32).astype(jnp.bfloat16),
        "head",
        scatter_dimension=0,
        tiled=True,
    ).astype(jnp.float32)
    gate_row = lax.dynamic_index_in_dim(gate_table, levels[0], 0, keepdims=True)
    return (hidden.astype(jnp.float32) + gate_row * projected).astype(jnp.bfloat16)


def solution(mesh):
    placed = (
        P(("group", "head"), None),
        P(("group", "head"), None),
        P(("group", "head"), None),
        P(("group", "head"), None),
        P("group", None),
        P("group"),
        P("head", None),
        P(),
    )
    return jax.shard_map(
        shards, mesh=mesh, in_specs=placed, out_specs=P(("group", "head"), None), check_vma=False
    )
```

profile of v0, /device:TPU:224, one launch (start us, length us, event | category | flops | bytes accessed | tf_op | source)
XLA Modules:
  0.0 930.6 jit_solution(12128387220531454086)
XLA Ops:
  8.3 4.5 all-to-all-start.2
  14.4 4.7 all-to-all-done.2
  24.2 4.6 all-to-all-done
  33.6 4.8 all-to-all-done.1
  41.0 777.8 %while.21 = (s32[]{:T(128)}, bf16[256,384]{0,1:T(8,128)(2,1)S(1)}, bf16[256,384]{0,1:T(8,128)(2,1)}, f32[3,256]{1,0:T(4,128)S(1)}, f32[3,256]{1,0:T(4,128)S(1)},...) while((s32[]{:T(128)}, bf16[256,384]{0,1:T(8,128)(2,1)S(1)}, ...), condition=%wide.region_5.6_spmd, body=%wide.region_2.5_spmd.sunk | while | flops 102630920 | bytes 6144277 | solution.py:75
  58.3 4.1 collective-permute-done
  70.7 4.1 collective-permute-done
  83.0 4.1 collective-permute-done
  95.4 4.1 collective-permute-done
  107.7 4.1 collective-permute-done
  120.1 4.1 collective-permute-done
  132.4 4.1 collective-permute-done
  144.8 4.1 collective-permute-done
  157.1 4.1 collective-permute-done
  169.5 4.1 collective-permute-done
  181.8 4.1 collective-permute-done
  194.2 4.1 collective-permute-done
  206.5 4.1 collective-permute-done
  218.9 4.1 collective-permute-done
  231.2 4.1 collective-permute-done
  243.5 4.1 collective-permute-done
  255.9 4.1 collective-permute-done
  268.2 4.1 collective-permute-done
  280.6 4.1 collective-permute-done
  292.9 4.1 collective-permute-done
  305.3 4.1 collective-permute-done
  317.6 4.1 collective-permute-done
  330.0 4.1 collective-permute-done
  342.3 4.1 collective-permute-done
  354.7 4.1 collective-permute-done
  367.0 4.1 collective-permute-done
  379.4 4.1 collective-permute-done
  391.7 4.1 collective-permute-done
  404.0 4.1 collective-permute-done
  416.4 4.1 collective-permute-done
  428.7 4.1 collective-permute-done
  441.1 4.1 collective-permute-done
  453.4 4.1 collective-permute-done
  465.8 4.1 collective-permute-done
  478.1 4.1 collective-permute-done
  490.5 4.1 collective-permute-done
  502.8 4.1 collective-permute-done
  515.2 4.1 collective-permute-done
  527.5 4.1 collective-permute-done
  539.9 4.1 collective-permute-done
  552.2 4.1 collective-permute-done
  564.6 4.1 collective-permute-done
  576.9 4.1 collective-permute-done
  589.2 4.1 collective-permute-done
  601.6 4.1 collective-permute-done
  613.9 4.1 collective-permute-done
  626.3 4.1 collective-permute-done
  638.6 4.1 collective-permute-done
  651.0 4.1 collective-permute-done
  663.3 4.1 collective-permute-done
  675.7 4.1 collective-permute-done
  688.0 4.1 collective-permute-done
  700.4 4.1 collective-permute-done
  712.7 4.1 collective-permute-done
  725.1 4.1 collective-permute-done
  749.7 4.1 collective-permute-done
  762.1 4.1 collective-permute-done
  811.5 4.1 collective-permute-done
  822.8 99.1 %reduce-scatter.2.cloned.1.call-done = bf16[64,3072]{1,0:T(8,128)(2,1)} async-done(((bf16[256,3072]{1,0:T(8,128)(2,1)}), bf16[64,3072]{1,0:T(8,128)(2,1)}) %reduce-scatter.2.cloned.1.call-update) | async-done | bytes 393232 | tf_op jit(solution)/shard_map/reduce_scatter | solution.py:84
  (792 shorter events, 522.1 us)
Async XLA Ops:
  8.3 10.8 %all-to-all-start.2 = ((bf16[64,4,384]{2,0,1:T(8,128)(2,1)}), bf16[64,4,384]{2,0,1:T(8,128)(2,1)S(1)}, u32[]{:S(2)}, u32[]{:S(2)}) async-start(bf16[64,4,384]{2,0,1:T(8,128)(2,1)} %bitcast.31), calls=%async_computation.2 | async-start | bytes 393216 | tf_op jit(solution)/shard_map/all_to_all | solution.py:17
  19.1 9.7 %all-to-all-start = ((bf16[64,4,384]{2,0,1:T(8,128)(2,1)}), bf16[64,4,384]{2,0,1:T(8,128)(2,1)S(1)}, u32[]{:S(2)}, u32[]{:S(2)}) async-start(bf16[64,4,384]{2,0,1:T(8,128)(2,1)} %bitcast.33), calls=%async_computation | async-start | bytes 393216 | tf_op jit(solution)/shard_map/all_to_all | solution.py:18
  28.8 9.7 %all-to-all-start.1 = ((bf16[64,4,384]{2,0,1:T(8,128)(2,1)}), bf16[64,4,384]{2,0,1:T(8,128)(2,1)S(1)}, u32[]{:S(2)}, u32[]{:S(2)}) async-start(bf16[64,4,384]{2,0,1:T(8,128)(2,1)} %bitcast.32), calls=%async_computation.1 | async-start | bytes 393216 | tf_op jit(solution)/shard_map/all_to_all | solution.py:19
  32.1 889.8 %reduce-scatter.2.cloned.1.call-start = ((), (), s32[]{:S(2)}) async-start(), calls=%async_computation.4 | async-start | bytes 1966080 | tf_op jit(solution)/shard_map/reduce_scatter | solution.py:84
  42.9 9.3 %collective-permute-start.1 = (bf16[256,384]{0,1:T(8,128)(2,1)}, bf16[256,384]{0,1:T(8,128)(2,1)S(1)}, u32[]{:S(2)}, u32[]{:S(2)}) collective-permute-start(bf16[256,384]{0,1:T(8,128)(2,1)} %get-tuple-element.302), channel_id=1, source_target_pairs={{0,4},{4,8},{8,12},{12,16},{16,20},{20,24},{24,28},{28,32},{32,36}... | collective-permute-start | bytes 589832 | tf_op jit(solution)/shard_map/while/body/eval_jaxpr/ppermute | solution.py:12
  55.3 9.3 %collective-permute-start.1 = (bf16[256,384]{0,1:T(8,128)(2,1)}, bf16[256,384]{0,1:T(8,128)(2,1)S(1)}, u32[]{:S(2)}, u32[]{:S(2)}) collective-permute-start(bf16[256,384]{0,1:T(8,128)(2,1)} %get-tuple-element.302), channel_id=1, source_target_pairs={{0,4},{4,8},{8,12},{12,16},{16,20},{20,24},{24,28},{28,32},{32,36}... | collective-permute-start | bytes 589832 | tf_op jit(solution)/shard_map/while/body/eval_jaxpr/ppermute | solution.py:12
  67.6 9.3 %collective-permute-start.1 = (bf16[256,384]{0,1:T(8,128)(2,1)}, bf16[256,384]{0,1:T(8,128)(2,1)S(1)}, u32[]{:S(2)}, u32[]{:S(2)}) collective-permute-start(bf16[256,384]{0,1:T(8,128)(2,1)} %get-tuple-element.302), channel_id=1, source_target_pairs={{0,4},{4,8},{8,12},{12,16},{16,20},{20,24},{24,28},{28,32},{32,36}... | collective-permute-start | bytes 589832 | tf_op jit(solution)/shard_map/while/body/eval_jaxpr/ppermute | solution.py:12
  80.0 9.3 %collective-permute-start.1 = (bf16[256,384]{0,1:T(8,128)(2,1)}, bf16[256,384]{0,1:T(8,128)(2,1)S(1)}, u32[]{:S(2)}, u32[]{:S(2)}) collective-permute-start(bf16[256,384]{0,1:T(8,128)(2,1)} %get-tuple-element.302), channel_id=1, source_target_pairs={{0,4},{4,8},{8,12},{12,16},{16,20},{20,24},{24,28},{28,32},{32,36}... | collective-permute-start | bytes 589832 | tf_op jit(solution)/shard_map/while/body/eval_jaxpr/ppermute | solution.py:12
  92.3 9.3 %collective-permute-start.1 = (bf16[256,384]{0,1:T(8,128)(2,1)}, bf16[256,384]{0,1:T(8,128)(2,1)S(1)}, u32[]{:S(2)}, u32[]{:S(2)}) collective-permute-start(bf16[256,384]{0,1:T(8,128)(2,1)} %get-tuple-element.302), channel_id=1, source_target_pairs={{0,4},{4,8},{8,12},{12,16},{16,20},{20,24},{24,28},{28,32},{32,36}... | collective-permute-start | bytes 589832 | tf_op jit(solution)/shard_map/while/body/eval_jaxpr/ppermute | solution.py:12
  104.6 9.3 %collective-permute-start.1 = (bf16[256,384]{0,1:T(8,128)(2,1)}, bf16[256,384]{0,1:T(8,128)(2,1)S(1)}, u32[]{:S(2)}, u32[]{:S(2)}) collective-permute-start(bf16[256,384]{0,1:T(8,128)(2,1)} %get-tuple-element.302), channel_id=1, source_target_pairs={{0,4},{4,8},{8,12},{12,16},{16,20},{20,24},{24,28},{28,32},{32,36}... | collective-permute-start | bytes 589832 | tf_op jit(solution)/shard_map/while/body/eval_jaxpr/ppermute | solution.py:12
  117.0 9.3 %collective-permute-start.1 = (bf16[256,384]{0,1:T(8,128)(2,1)}, bf16[256,384]{0,1:T(8,128)(2,1)S(1)}, u32[]{:S(2)}, u32[]{:S(2)}) collective-permute-start(bf16[256,384]{0,1:T(8,128)(2,1)} %get-tuple-element.302), channel_id=1, source_target_pairs={{0,4},{4,8},{8,12},{12,16},{16,20},{20,24},{24,28},{28,32},{32,36}... | collective-permute-start | bytes 589832 | tf_op jit(solution)/shard_map/while/body/eval_jaxpr/ppermute | solution.py:12
  129.3 9.3 %collective-permute-start.1 = (bf16[256,384]{0,1:T(8,128)(2,1)}, bf16[256,384]{0,1:T(8,128)(2,1)S(1)}, u32[]{:S(2)}, u32[]{:S(2)}) collective-permute-start(bf16[256,384]{0,1:T(8,128)(2,1)} %get-tuple-element.302), channel_id=1, source_target_pairs={{0,4},{4,8},{8,12},{12,16},{16,20},{20,24},{24,28},{28,32},{32,36}... | collective-permute-start | bytes 589832 | tf_op jit(solution)/shard_map/while/body/eval_jaxpr/ppermute | solution.py:12
  141.7 9.3 %collective-permute-start.1 = (bf16[256,384]{0,1:T(8,128)(2,1)}, bf16[256,384]{0,1:T(8,128)(2,1)S(1)}, u32[]{:S(2)}, u32[]{:S(2)}) collective-permute-start(bf16[256,384]{0,1:T(8,128)(2,1)} %get-tuple-element.302), channel_id=1, source_target_pairs={{0,4},{4,8},{8,12},{12,16},{16,20},{20,24},{24,28},{28,32},{32,36}... | collective-permute-start | bytes 589832 | tf_op jit(solution)/shard_map/while/body/eval_jaxpr/ppermute | solution.py:12
  154.0 9.3 %collective-permute-start.1 = (bf16[256,384]{0,1:T(8,128)(2,1)}, bf16[256,384]{0,1:T(8,128)(2,1)S(1)}, u32[]{:S(2)}, u32[]{:S(2)}) collective-permute-start(bf16[256,384]{0,1:T(8,128)(2,1)} %get-tuple-element.302), channel_id=1, source_target_pairs={{0,4},{4,8},{8,12},{12,16},{16,20},{20,24},{24,28},{28,32},{32,36}... | collective-permute-start | bytes 589832 | tf_op jit(solution)/shard_map/while/body/eval_jaxpr/ppermute | solution.py:12
  166.4 9.3 %collective-permute-start.1 = (bf16[256,384]{0,1:T(8,128)(2,1)}, bf16[256,384]{0,1:T(8,128)(2,1)S(1)}, u32[]{:S(2)}, u32[]{:S(2)}) collective-permute-start(bf16[256,384]{0,1:T(8,128)(2,1)} %get-tuple-element.302), channel_id=1, source_target_pairs={{0,4},{4,8},{8,12},{12,16},{16,20},{20,24},{24,28},{28,32},{32,36}... | collective-permute-start | bytes 589832 | tf_op jit(solution)/shard_map/while/body/eval_jaxpr/ppermute | solution.py:12
  178.7 9.3 %collective-permute-start.1 = (bf16[256,384]{0,1:T(8,128)(2,1)}, bf16[256,384]{0,1:T(8,128)(2,1)S(1)}, u32[]{:S(2)}, u32[]{:S(2)}) collective-permute-start(bf16[256,384]{0,1:T(8,128)(2,1)} %get-tuple-element.302), channel_id=1, source_target_pairs={{0,4},{4,8},{8,12},{12,16},{16,20},{20,24},{24,28},{28,32},{32,36}... | collective-permute-start | bytes 589832 | tf_op jit(solution)/shard_map/while/body/eval_jaxpr/ppermute | solution.py:12
  191.1 9.3 %collective-permute-start.1 = (bf16[256,384]{0,1:T(8,128)(2,1)}, bf16[256,384]{0,1:T(8,128)(2,1)S(1)}, u32[]{:S(2)}, u32[]{:S(2)}) collective-permute-start(bf16[256,384]{0,1:T(8,128)(2,1)} %get-tuple-element.302), channel_id=1, source_target_pairs={{0,4},{4,8},{8,12},{12,16},{16,20},{20,24},{24,28},{28,32},{32,36}... | collective-permute-start | bytes 589832 | tf_op jit(solution)/shard_map/while/body/eval_jaxpr/ppermute | solution.py:12
  203.4 9.3 %collective-permute-start.1 = (bf16[256,384]{0,1:T(8,128)(2,1)}, bf16[256,384]{0,1:T(8,128)(2,1)S(1)}, u32[]{:S(2)}, u32[]{:S(2)}) collective-permute-start(bf16[256,384]{0,1:T(8,128)(2,1)} %get-tuple-element.302), channel_id=1, source_target_pairs={{0,4},{4,8},{8,12},{12,16},{16,20},{20,24},{24,28},{28,32},{32,36}... | collective-permute-start | bytes 589832 | tf_op jit(solution)/shard_map/while/body/eval_jaxpr/ppermute | solution.py:12
  215.8 9.3 %collective-permute-start.1 = (bf16[256,384]{0,1:T(8,128)(2,1)}, bf16[256,384]{0,1:T(8,128)(2,1)S(1)}, u32[]{:S(2)}, u32[]{:S(2)}) collective-permute-start(bf16[256,384]{0,1:T(8,128)(2,1)} %get-tuple-element.302), channel_id=1, source_target_pairs={{0,4},{4,8},{8,12},{12,16},{16,20},{20,24},{24,28},{28,32},{32,36}... | collective-permute-start | bytes 589832 | tf_op jit(solution)/shard_map/while/body/eval_jaxpr/ppermute | solution.py:12
  228.1 9.3 %collective-permute-start.1 = (bf16[256,384]{0,1:T(8,128)(2,1)}, bf16[256,384]{0,1:T(8,128)(2,1)S(1)}, u32[]{:S(2)}, u32[]{:S(2)}) collective-permute-start(bf16[256,384]{0,1:T(8,128)(2,1)} %get-tuple-element.302), channel_id=1, source_target_pairs={{0,4},{4,8},{8,12},{12,16},{16,20},{20,24},{24,28},{28,32},{32,36}... | collective-permute-start | bytes 589832 | tf_op jit(solution)/shard_map/while/body/eval_jaxpr/ppermute | solution.py:12
  240.5 9.3 %collective-permute-start.1 = (bf16[256,384]{0,1:T(8,128)(2,1)}, bf16[256,384]{0,1:T(8,128)(2,1)S(1)}, u32[]{:S(2)}, u32[]{:S(2)}) collective-permute-start(bf16[256,384]{0,1:T(8,128)(2,1)} %get-tuple-element.302), channel_id=1, source_target_pairs={{0,4},{4,8},{8,12},{12,16},{16,20},{20,24},{24,28},{28,32},{32,36}... | collective-permute-start | bytes 589832 | tf_op jit(solution)/shard_map/while/body/eval_jaxpr/ppermute | solution.py:12
  252.8 9.3 %collective-permute-start.1 = (bf16[256,384]{0,1:T(8,128)(2,1)}, bf16[256,384]{0,1:T(8,128)(2,1)S(1)}, u32[]{:S(2)}, u32[]{:S(2)}) collective-permute-start(bf16[256,384]{0,1:T(8,128)(2,1)} %get-tuple-element.302), channel_id=1, source_target_pairs={{0,4},{4,8},{8,12},{12,16},{16,20},{20,24},{24,28},{28,32},{32,36}... | collective-permute-start | bytes 589832 | tf_op jit(solution)/shard_map/while/body/eval_jaxpr/ppermute | solution.py:12
  265.1 9.3 %collective-permute-start.1 = (bf16[256,384]{0,1:T(8,128)(2,1)}, bf16[256,384]{0,1:T(8,128)(2,1)S(1)}, u32[]{:S(2)}, u32[]{:S(2)}) collective-permute-start(bf16[256,384]{0,1:T(8,128)(2,1)} %get-tuple-element.302), channel_id=1, source_target_pairs={{0,4},{4,8},{8,12},{12,16},{16,20},{20,24},{24,28},{28,32},{32,36}... | collective-permute-start | bytes 589832 | tf_op jit(solution)/shard_map/while/body/eval_jaxpr/ppermute | solution.py:12
  277.5 9.3 %collective-permute-start.1 = (bf16[256,384]{0,1:T(8,128)(2,1)}, bf16[256,384]{0,1:T(8,128)(2,1)S(1)}, u32[]{:S(2)}, u32[]{:S(2)}) collective-permute-start(bf16[256,384]{0,1:T(8,128)(2,1)} %get-tuple-element.302), channel_id=1, source_target_pairs={{0,4},{4,8},{8,12},{12,16},{16,20},{20,24},{24,28},{28,32},{32,36}... | collective-permute-start | bytes 589832 | tf_op jit(solution)/shard_map/while/body/eval_jaxpr/ppermute | solution.py:12
  289.8 9.3 %collective-permute-start.1 = (bf16[256,384]{0,1:T(8,128)(2,1)}, bf16[256,384]{0,1:T(8,128)(2,1)S(1)}, u32[]{:S(2)}, u32[]{:S(2)}) collective-permute-start(bf16[256,384]{0,1:T(8,128)(2,1)} %get-tuple-element.302), channel_id=1, source_target_pairs={{0,4},{4,8},{8,12},{12,16},{16,20},{20,24},{24,28},{28,32},{32,36}... | collective-permute-start | bytes 589832 | tf_op jit(solution)/shard_map/while/body/eval_jaxpr/ppermute | solution.py:12
  302.2 9.3 %collective-permute-start.1 = (bf16[256,384]{0,1:T(8,128)(2,1)}, bf16[256,384]{0,1:T(8,128)(2,1)S(1)}, u32[]{:S(2)}, u32[]{:S(2)}) collective-permute-start(bf16[256,384]{0,1:T(8,128)(2,1)} %get-tuple-element.302), channel_id=1, source_target_pairs={{0,4},{4,8},{8,12},{12,16},{16,20},{20,24},{24,28},{28,32},{32,36}... | collective-permute-start | bytes 589832 | tf_op jit(solution)/shard_map/while/body/eval_jaxpr/ppermute | solution.py:12
  314.5 9.3 %collective-permute-start.1 = (bf16[256,384]{0,1:T(8,128)(2,1)}, bf16[256,384]{0,1:T(8,128)(2,1)S(1)}, u32[]{:S(2)}, u32[]{:S(2)}) collective-permute-start(bf16[256,384]{0,1:T(8,128)(2,1)} %get-tuple-element.302), channel_id=1, source_target_pairs={{0,4},{4,8},{8,12},{12,16},{16,20},{20,24},{24,28},{28,32},{32,36}... | collective-permute-start | bytes 589832 | tf_op jit(solution)/shard_map/while/body/eval_jaxpr/ppermute | solution.py:12
  326.9 9.3 %collective-permute-start.1 = (bf16[256,384]{0,1:T(8,128)(2,1)}, bf16[256,384]{0,1:T(8,128)(2,1)S(1)}, u32[]{:S(2)}, u32[]{:S(2)}) collective-permute-start(bf16[256,384]{0,1:T(8,128)(2,1)} %get-tuple-element.302), channel_id=1, source_target_pairs={{0,4},{4,8},{8,12},{12,16},{16,20},{20,24},{24,28},{28,32},{32,36}... | collective-permute-start | bytes 589832 | tf_op jit(solution)/shard_map/while/body/eval_jaxpr/ppermute | solution.py:12
  339.2 9.3 %collective-permute-start.1 = (bf16[256,384]{0,1:T(8,128)(2,1)}, bf16[256,384]{0,1:T(8,128)(2,1)S(1)}, u32[]{:S(2)}, u32[]{:S(2)}) collective-permute-start(bf16[256,384]{0,1:T(8,128)(2,1)} %get-tuple-element.302), channel_id=1, source_target_pairs={{0,4},{4,8},{8,12},{12,16},{16,20},{20,24},{24,28},{28,32},{32,36}... | collective-permute-start | bytes 589832 | tf_op jit(solution)/shard_map/while/body/eval_jaxpr/ppermute | solution.py:12
  351.6 9.3 %collective-permute-start.1 = (bf16[256,384]{0,1:T(8,128)(2,1)}, bf16[256,384]{0,1:T(8,128)(2,1)S(1)}, u32[]{:S(2)}, u32[]{:S(2)}) collective-permute-start(bf16[256,384]{0,1:T(8,128)(2,1)} %get-tuple-element.302), channel_id=1, source_target_pairs={{0,4},{4,8},{8,12},{12,16},{16,20},{20,24},{24,28},{28,32},{32,36}... | collective-permute-start | bytes 589832 | tf_op jit(solution)/shard_map/while/body/eval_jaxpr/ppermute | solution.py:12
  363.9 9.3 %collective-permute-start.1 = (bf16[256,384]{0,1:T(8,128)(2,1)}, bf16[256,384]{0,1:T(8,128)(2,1)S(1)}, u32[]{:S(2)}, u32[]{:S(2)}) collective-permute-start(bf16[256,384]{0,1:T(8,128)(2,1)} %get-tuple-element.302), channel_id=1, source_target_pairs={{0,4},{4,8},{8,12},{12,16},{16,20},{20,24},{24,28},{28,32},{32,36}... | collective-permute-start | bytes 589832 | tf_op jit(solution)/shard_map/while/body/eval_jaxpr/ppermute | solution.py:12
  376.3 9.3 %collective-permute-start.1 = (bf16[256,384]{0,1:T(8,128)(2,1)}, bf16[256,384]{0,1:T(8,128)(2,1)S(1)}, u32[]{:S(2)}, u32[]{:S(2)}) collective-permute-start(bf16[256,384]{0,1:T(8,128)(2,1)} %get-tuple-element.302), channel_id=1, source_target_pairs={{0,4},{4,8},{8,12},{12,16},{16,20},{20,24},{24,28},{28,32},{32,36}... | collective-permute-start | bytes 589832 | tf_op jit(solution)/shard_map/while/body/eval_jaxpr/ppermute | solution.py:12
  388.6 9.3 %collective-permute-start.1 = (bf16[256,384]{0,1:T(8,128)(2,1)}, bf16[256,384]{0,1:T(8,128)(2,1)S(1)}, u32[]{:S(2)}, u32[]{:S(2)}) collective-permute-start(bf16[256,384]{0,1:T(8,128)(2,1)} %get-tuple-element.302), channel_id=1, source_target_pairs={{0,4},{4,8},{8,12},{12,16},{16,20},{20,24},{24,28},{28,32},{32,36}... | collective-permute-start | bytes 589832 | tf_op jit(solution)/shard_map/while/body/eval_jaxpr/ppermute | solution.py:12
  401.0 9.3 %collective-permute-start.1 = (bf16[256,384]{0,1:T(8,128)(2,1)}, bf16[256,384]{0,1:T(8,128)(2,1)S(1)}, u32[]{:S(2)}, u32[]{:S(2)}) collective-permute-start(bf16[256,384]{0,1:T(8,128)(2,1)} %get-tuple-element.302), channel_id=1, source_target_pairs={{0,4},{4,8},{8,12},{12,16},{16,20},{20,24},{24,28},{28,32},{32,36}... | collective-permute-start | bytes 589832 | tf_op jit(solution)/shard_map/while/body/eval_jaxpr/ppermute | solution.py:12
  413.3 9.3 %collective-permute-start.1 = (bf16[256,384]{0,1:T(8,128)(2,1)}, bf16[256,384]{0,1:T(8,128)(2,1)S(1)}, u32[]{:S(2)}, u32[]{:S(2)}) collective-permute-start(bf16[256,384]{0,1:T(8,128)(2,1)} %get-tuple-element.302), channel_id=1, source_target_pairs={{0,4},{4,8},{8,12},{12,16},{16,20},{20,24},{24,28},{28,32},{32,36}... | collective-permute-start | bytes 589832 | tf_op jit(solution)/shard_map/while/body/eval_jaxpr/ppermute | solution.py:12
  425.7 9.3 %collective-permute-start.1 = (bf16[256,384]{0,1:T(8,128)(2,1)}, bf16[256,384]{0,1:T(8,128)(2,1)S(1)}, u32[]{:S(2)}, u32[]{:S(2)}) collective-permute-start(bf16[256,384]{0,1:T(8,128)(2,1)} %get-tuple-element.302), channel_id=1, source_target_pairs={{0,4},{4,8},{8,12},{12,16},{16,20},{20,24},{24,28},{28,32},{32,36}... | collective-permute-start | bytes 589832 | tf_op jit(solution)/shard_map/while/body/eval_jaxpr/ppermute | solution.py:12
  438.0 9.3 %collective-permute-start.1 = (bf16[256,384]{0,1:T(8,128)(2,1)}, bf16[256,384]{0,1:T(8,128)(2,1)S(1)}, u32[]{:S(2)}, u32[]{:S(2)}) collective-permute-start(bf16[256,384]{0,1:T(8,128)(2,1)} %get-tuple-element.302), channel_id=1, source_target_pairs={{0,4},{4,8},{8,12},{12,16},{16,20},{20,24},{24,28},{28,32},{32,36}... | collective-permute-start | bytes 589832 | tf_op jit(solution)/shard_map/while/body/eval_jaxpr/ppermute | solution.py:12
  450.3 9.3 %collective-permute-start.1 = (bf16[256,384]{0,1:T(8,128)(2,1)}, bf16[256,384]{0,1:T(8,128)(2,1)S(1)}, u32[]{:S(2)}, u32[]{:S(2)}) collective-permute-start(bf16[256,384]{0,1:T(8,128)(2,1)} %get-tuple-element.302), channel_id=1, source_target_pairs={{0,4},{4,8},{8,12},{12,16},{16,20},{20,24},{24,28},{28,32},{32,36}... | collective-permute-start | bytes 589832 | tf_op jit(solution)/shard_map/while/body/eval_jaxpr/ppermute | solution.py:12
  462.7 9.3 %collective-permute-start.1 = (bf16[256,384]{0,1:T(8,128)(2,1)}, bf16[256,384]{0,1:T(8,128)(2,1)S(1)}, u32[]{:S(2)}, u32[]{:S(2)}) collective-permute-start(bf16[256,384]{0,1:T(8,128)(2,1)} %get-tuple-element.302), channel_id=1, source_target_pairs={{0,4},{4,8},{8,12},{12,16},{16,20},{20,24},{24,28},{28,32},{32,36}... | collective-permute-start | bytes 589832 | tf_op jit(solution)/shard_map/while/body/eval_jaxpr/ppermute | solution.py:12
  475.0 9.3 %collective-permute-start.1 = (bf16[256,384]{0,1:T(8,128)(2,1)}, bf16[256,384]{0,1:T(8,128)(2,1)S(1)}, u32[]{:S(2)}, u32[]{:S(2)}) collective-permute-start(bf16[256,384]{0,1:T(8,128)(2,1)} %get-tuple-element.302), channel_id=1, source_target_pairs={{0,4},{4,8},{8,12},{12,16},{16,20},{20,24},{24,28},{28,32},{32,36}... | collective-permute-start | bytes 589832 | tf_op jit(solution)/shard_map/while/body/eval_jaxpr/ppermute | solution.py:12
  487.4 9.3 %collective-permute-start.1 = (bf16[256,384]{0,1:T(8,128)(2,1)}, bf16[256,384]{0,1:T(8,128)(2,1)S(1)}, u32[]{:S(2)}, u32[]{:S(2)}) collective-permute-start(bf16[256,384]{0,1:T(8,128)(2,1)} %get-tuple-element.302), channel_id=1, source_target_pairs={{0,4},{4,8},{8,12},{12,16},{16,20},{20,24},{24,28},{28,32},{32,36}... | collective-permute-start | bytes 589832 | tf_op jit(solution)/shard_map/while/body/eval_jaxpr/ppermute | solution.py:12
  499.7 9.3 %collective-permute-start.1 = (bf16[256,384]{0,1:T(8,128)(2,1)}, bf16[256,384]{0,1:T(8,128)(2,1)S(1)}, u32[]{:S(2)}, u32[]{:S(2)}) collective-permute-start(bf16[256,384]{0,1:T(8,128)(2,1)} %get-tuple-element.302), channel_id=1, source_target_pairs={{0,4},{4,8},{8,12},{12,16},{16,20},{20,24},{24,28},{28,32},{32,36}... | collective-permute-start | bytes 589832 | tf_op jit(solution)/shard_map/while/body/eval_jaxpr/ppermute | solution.py:12
  512.1 9.3 %collective-permute-start.1 = (bf16[256,384]{0,1:T(8,128)(2,1)}, bf16[256,384]{0,1:T(8,128)(2,1)S(1)}, u32[]{:S(2)}, u32[]{:S(2)}) collective-permute-start(bf16[256,384]{0,1:T(8,128)(2,1)} %get-tuple-element.302), channel_id=1, source_target_pairs={{0,4},{4,8},{8,12},{12,16},{16,20},{20,24},{24,28},{28,32},{32,36}... | collective-permute-start | bytes 589832 | tf_op jit(solution)/shard_map/while/body/eval_jaxpr/ppermute | solution.py:12
  524.4 9.3 %collective-permute-start.1 = (bf16[256,384]{0,1:T(8,128)(2,1)}, bf16[256,384]{0,1:T(8,128)(2,1)S(1)}, u32[]{:S(2)}, u32[]{:S(2)}) collective-permute-start(bf16[256,384]{0,1:T(8,128)(2,1)} %get-tuple-element.302), channel_id=1, source_target_pairs={{0,4},{4,8},{8,12},{12,16},{16,20},{20,24},{24,28},{28,32},{32,36}... | collective-permute-start | bytes 589832 | tf_op jit(solution)/shard_map/while/body/eval_jaxpr/ppermute | solution.py:12
  536.8 9.3 %collective-permute-start.1 = (bf16[256,384]{0,1:T(8,128)(2,1)}, bf16[256,384]{0,1:T(8,128)(2,1)S(1)}, u32[]{:S(2)}, u32[]{:S(2)}) collective-permute-start(bf16[256,384]{0,1:T(8,128)(2,1)} %get-tuple-element.302), channel_id=1, source_target_pairs={{0,4},{4,8},{8,12},{12,16},{16,20},{20,24},{24,28},{28,32},{32,36}... | collective-permute-start | bytes 589832 | tf_op jit(solution)/shard_map/while/body/eval_jaxpr/ppermute | solution.py:12
  549.1 9.3 %collective-permute-start.1 = (bf16[256,384]{0,1:T(8,128)(2,1)}, bf16[256,384]{0,1:T(8,128)(2,1)S(1)}, u32[]{:S(2)}, u32[]{:S(2)}) collective-permute-start(bf16[256,384]{0,1:T(8,128)(2,1)} %get-tuple-element.302), channel_id=1, source_target_pairs={{0,4},{4,8},{8,12},{12,16},{16,20},{20,24},{24,28},{28,32},{32,36}... | collective-permute-start | bytes 589832 | tf_op jit(solution)/shard_map/while/body/eval_jaxpr/ppermute | solution.py:12
  561.5 9.3 %collective-permute-start.1 = (bf16[256,384]{0,1:T(8,128)(2,1)}, bf16[256,384]{0,1:T(8,128)(2,1)S(1)}, u32[]{:S(2)}, u32[]{:S(2)}) collective-permute-start(bf16[256,384]{0,1:T(8,128)(2,1)} %get-tuple-element.302), channel_id=1, source_target_pairs={{0,4},{4,8},{8,12},{12,16},{16,20},{20,24},{24,28},{28,32},{32,36}... | collective-permute-start | bytes 589832 | tf_op jit(solution)/shard_map/while/body/eval_jaxpr/ppermute | solution.py:12
  573.8 9.3 %collective-permute-start.1 = (bf16[256,384]{0,1:T(8,128)(2,1)}, bf16[256,384]{0,1:T(8,128)(2,1)S(1)}, u32[]{:S(2)}, u32[]{:S(2)}) collective-permute-start(bf16[256,384]{0,1:T(8,128)(2,1)} %get-tuple-element.302), channel_id=1, source_target_pairs={{0,4},{4,8},{8,12},{12,16},{16,20},{20,24},{24,28},{28,32},{32,36}... | collective-permute-start | bytes 589832 | tf_op jit(solution)/shard_map/while/body/eval_jaxpr/ppermute | solution.py:12
  586.2 9.3 %collective-permute-start.1 = (bf16[256,384]{0,1:T(8,128)(2,1)}, bf16[256,384]{0,1:T(8,128)(2,1)S(1)}, u32[]{:S(2)}, u32[]{:S(2)}) collective-permute-start(bf16[256,384]{0,1:T(8,128)(2,1)} %get-tuple-element.302), channel_id=1, source_target_pairs={{0,4},{4,8},{8,12},{12,16},{16,20},{20,24},{24,28},{28,32},{32,36}... | collective-permute-start | bytes 589832 | tf_op jit(solution)/shard_map/while/body/eval_jaxpr/ppermute | solution.py:12
  598.5 9.3 %collective-permute-start.1 = (bf16[256,384]{0,1:T(8,128)(2,1)}, bf16[256,384]{0,1:T(8,128)(2,1)S(1)}, u32[]{:S(2)}, u32[]{:S(2)}) collective-permute-start(bf16[256,384]{0,1:T(8,128)(2,1)} %get-tuple-element.302), channel_id=1, source_target_pairs={{0,4},{4,8},{8,12},{12,16},{16,20},{20,24},{24,28},{28,32},{32,36}... | collective-permute-start | bytes 589832 | tf_op jit(solution)/shard_map/while/body/eval_jaxpr/ppermute | solution.py:12
  610.8 9.3 %collective-permute-start.1 = (bf16[256,384]{0,1:T(8,128)(2,1)}, bf16[256,384]{0,1:T(8,128)(2,1)S(1)}, u32[]{:S(2)}, u32[]{:S(2)}) collective-permute-start(bf16[256,384]{0,1:T(8,128)(2,1)} %get-tuple-element.302), channel_id=1, source_target_pairs={{0,4},{4,8},{8,12},{12,16},{16,20},{20,24},{24,28},{28,32},{32,36}... | collective-permute-start | bytes 589832 | tf_op jit(solution)/shard_map/while/body/eval_jaxpr/ppermute | solution.py:12
  623.2 9.3 %collective-permute-start.1 = (bf16[256,384]{0,1:T(8,128)(2,1)}, bf16[256,384]{0,1:T(8,128)(2,1)S(1)}, u32[]{:S(2)}, u32[]{:S(2)}) collective-permute-start(bf16[256,384]{0,1:T(8,128)(2,1)} %get-tuple-element.302), channel_id=1, source_target_pairs={{0,4},{4,8},{8,12},{12,16},{16,20},{20,24},{24,28},{28,32},{32,36}... | collective-permute-start | bytes 589832 | tf_op jit(solution)/shard_map/while/body/eval_jaxpr/ppermute | solution.py:12
  635.5 9.3 %collective-permute-start.1 = (bf16[256,384]{0,1:T(8,128)(2,1)}, bf16[256,384]{0,1:T(8,128)(2,1)S(1)}, u32[]{:S(2)}, u32[]{:S(2)}) collective-permute-start(bf16[256,384]{0,1:T(8,128)(2,1)} %get-tuple-element.302), channel_id=1, source_target_pairs={{0,4},{4,8},{8,12},{12,16},{16,20},{20,24},{24,28},{28,32},{32,36}... | collective-permute-start | bytes 589832 | tf_op jit(solution)/shard_map/while/body/eval_jaxpr/ppermute | solution.py:12
  647.9 9.3 %collective-permute-start.1 = (bf16[256,384]{0,1:T(8,128)(2,1)}, bf16[256,384]{0,1:T(8,128)(2,1)S(1)}, u32[]{:S(2)}, u32[]{:S(2)}) collective-permute-start(bf16[256,384]{0,1:T(8,128)(2,1)} %get-tuple-element.302), channel_id=1, source_target_pairs={{0,4},{4,8},{8,12},{12,16},{16,20},{20,24},{24,28},{28,32},{32,36}... | collective-permute-start | bytes 589832 | tf_op jit(solution)/shard_map/while/body/eval_jaxpr/ppermute | solution.py:12
  660.2 9.3 %collective-permute-start.1 = (bf16[256,384]{0,1:T(8,128)(2,1)}, bf16[256,384]{0,1:T(8,128)(2,1)S(1)}, u32[]{:S(2)}, u32[]{:S(2)}) collective-permute-start(bf16[256,384]{0,1:T(8,128)(2,1)} %get-tuple-element.302), channel_id=1, source_target_pairs={{0,4},{4,8},{8,12},{12,16},{16,20},{20,24},{24,28},{28,32},{32,36}... | collective-permute-start | bytes 589832 | tf_op jit(solution)/shard_map/while/body/eval_jaxpr/ppermute | solution.py:12
  672.6 9.3 %collective-permute-start.1 = (bf16[256,384]{0,1:T(8,128)(2,1)}, bf16[256,384]{0,1:T(8,128)(2,1)S(1)}, u32[]{:S(2)}, u32[]{:S(2)}) collective-permute-start(bf16[256,384]{0,1:T(8,128)(2,1)} %get-tuple-element.302), channel_id=1, source_target_pairs={{0,4},{4,8},{8,12},{12,16},{16,20},{20,24},{24,28},{28,32},{32,36}... | collective-permute-start | bytes 589832 | tf_op jit(solution)/shard_map/while/body/eval_jaxpr/ppermute | solution.py:12
  684.9 9.3 %collective-permute-start.1 = (bf16[256,384]{0,1:T(8,128)(2,1)}, bf16[256,384]{0,1:T(8,128)(2,1)S(1)}, u32[]{:S(2)}, u32[]{:S(2)}) collective-permute-start(bf16[256,384]{0,1:T(8,128)(2,1)} %get-tuple-element.302), channel_id=1, source_target_pairs={{0,4},{4,8},{8,12},{12,16},{16,20},{20,24},{24,28},{28,32},{32,36}... | collective-permute-start | bytes 589832 | tf_op jit(solution)/shard_map/while/body/eval_jaxpr/ppermute | solution.py:12
  697.3 9.3 %collective-permute-start.1 = (bf16[256,384]{0,1:T(8,128)(2,1)}, bf16[256,384]{0,1:T(8,128)(2,1)S(1)}, u32[]{:S(2)}, u32[]{:S(2)}) collective-permute-start(bf16[256,384]{0,1:T(8,128)(2,1)} %get-tuple-element.302), channel_id=1, source_target_pairs={{0,4},{4,8},{8,12},{12,16},{16,20},{20,24},{24,28},{28,32},{32,36}... | collective-permute-start | bytes 589832 | tf_op jit(solution)/shard_map/while/body/eval_jaxpr/ppermute | solution.py:12
  709.6 9.3 %collective-permute-start.1 = (bf16[256,384]{0,1:T(8,128)(2,1)}, bf16[256,384]{0,1:T(8,128)(2,1)S(1)}, u32[]{:S(2)}, u32[]{:S(2)}) collective-permute-start(bf16[256,384]{0,1:T(8,128)(2,1)} %get-tuple-element.302), channel_id=1, source_target_pairs={{0,4},{4,8},{8,12},{12,16},{16,20},{20,24},{24,28},{28,32},{32,36}... | collective-permute-start | bytes 589832 | tf_op jit(solution)/shard_map/while/body/eval_jaxpr/ppermute | solution.py:12
  722.0 9.3 %collective-permute-start.1 = (bf16[256,384]{0,1:T(8,128)(2,1)}, bf16[256,384]{0,1:T(8,128)(2,1)S(1)}, u32[]{:S(2)}, u32[]{:S(2)}) collective-permute-start(bf16[256,384]{0,1:T(8,128)(2,1)} %get-tuple-element.302), channel_id=1, source_target_pairs={{0,4},{4,8},{8,12},{12,16},{16,20},{20,24},{24,28},{28,32},{32,36}... | collective-permute-start | bytes 589832 | tf_op jit(solution)/shard_map/while/body/eval_jaxpr/ppermute | solution.py:12
  734.3 9.3 %collective-permute-start.1 = (bf16[256,384]{0,1:T(8,128)(2,1)}, bf16[256,384]{0,1:T(8,128)(2,1)S(1)}, u32[]{:S(2)}, u32[]{:S(2)}) collective-permute-start(bf16[256,384]{0,1:T(8,128)(2,1)} %get-tuple-element.302), channel_id=1, source_target_pairs={{0,4},{4,8},{8,12},{12,16},{16,20},{20,24},{24,28},{28,32},{32,36}... | collective-permute-start | bytes 589832 | tf_op jit(solution)/shard_map/while/body/eval_jaxpr/ppermute | solution.py:12
  746.7 9.3 %collective-permute-start.1 = (bf16[256,384]{0,1:T(8,128)(2,1)}, bf16[256,384]{0,1:T(8,128)(2,1)S(1)}, u32[]{:S(2)}, u32[]{:S(2)}) collective-permute-start(bf16[256,384]{0,1:T(8,128)(2,1)} %get-tuple-element.302), channel_id=1, source_target_pairs={{0,4},{4,8},{8,12},{12,16},{16,20},{20,24},{24,28},{28,32},{32,36}... | collective-permute-start | bytes 589832 | tf_op jit(solution)/shard_map/while/body/eval_jaxpr/ppermute | solution.py:12
  759.0 9.3 %collective-permute-start.1 = (bf16[256,384]{0,1:T(8,128)(2,1)}, bf16[256,384]{0,1:T(8,128)(2,1)S(1)}, u32[]{:S(2)}, u32[]{:S(2)}) collective-permute-start(bf16[256,384]{0,1:T(8,128)(2,1)} %get-tuple-element.302), channel_id=1, source_target_pairs={{0,4},{4,8},{8,12},{12,16},{16,20},{20,24},{24,28},{28,32},{32,36}... | collective-permute-start | bytes 589832 | tf_op jit(solution)/shard_map/while/body/eval_jaxpr/ppermute | solution.py:12
  771.4 9.3 %collective-permute-start.1 = (bf16[256,384]{0,1:T(8,128)(2,1)}, bf16[256,384]{0,1:T(8,128)(2,1)S(1)}, u32[]{:S(2)}, u32[]{:S(2)}) collective-permute-start(bf16[256,384]{0,1:T(8,128)(2,1)} %get-tuple-element.302), channel_id=1, source_target_pairs={{0,4},{4,8},{8,12},{12,16},{16,20},{20,24},{24,28},{28,32},{32,36}... | collective-permute-start | bytes 589832 | tf_op jit(solution)/shard_map/while/body/eval_jaxpr/ppermute | solution.py:12
  (70 other events, 1525.4 us)
Sparse Core Ops, SparseCore 0:
  821.4 100.4 reduce-scatter.1
where the time goes:
time: 938 us; the launch traced here: 931 us
  waiting for transfers between devices  471 us (50%)
  starting transfers between devices  254 us (27%)
  local copies, waits for them, and re-layouts  88.6 us (9%)
  matrix products  50.4 us (5%)
  loops' own time  40 us (4%)
  between operations  14.2 us (2%)
  other arithmetic  12.8 us (1%)
    ppermute x126, waiting for transfers between devices, from_behind(): return lax.ppermute(block, axis, route)  357 us
    ppermute x126, starting transfers between devices, from_behind(): return lax.ppermute(block, axis, route)  243 us
    reduce_scatter x1, waiting for transfers between devices, shards(): lax.psum_scatter(jnp.dot(attended, out_weight, preferred_element_type=jnp...  99.1 us
    while x189, local copies, waits for them, and re-layouts  43.9 us
    another operation x1, loops' own time, shards(): lax.fori_loop(1, lax.axis_size('group'), chain_step, ((local_keys, local_...  40 us
    dynamic_slice x63, local copies, waits for them, and re-layouts, chain_step(): lax.dynamic_index_in_dim(attend_row, clipped, 0, keepdims=False) > 0  36.5 us
    dot_general x64, matrix products, absorb(): jnp.einsum('hqk,khd->hqd', weights.astype(jnp.bfloat16), value_three, pre...  27.6 us
    dot_general x64, matrix products, absorb(): jnp.einsum('qhd,khd->hqk', query_three, key_three, preferred_element_type...  20.6 us
  transfers between devices with their start and end apart: 130, of which 130 were waited for; matrix products, arithmetic and copies ran while one was open for 8% of the time, Pallas kernels for 0%

commit v1 on v0

v1 whole, which is shorter than its diff:
```python
import functools

import jax
import jax.numpy as jnp
from jax import lax
from jax.experimental import pallas as pl
from jax.experimental.pallas import tpu as pltpu
from jax.sharding import Mesh, PartitionSpec as P

HS = 128
NZ, NX, NC, NY = 8, 4, 2, 4
GROUPS = 64
ROWS = 256
PART = 64
WIDTH = 384
HEADS = WIDTH // HS
D = 3072
SCALE = 1.4426950408889634 * HS**-0.5
NONE = -1e30
MESH_ID = pl.DeviceIdType.MESH


def attention_kernel(
    q_hbm, k_hbm, v_hbm, bias_in, out_hbm,
    qin, vin, kbuf, vbuf, qt, bias, acc, top, total, osend, orecv, ssend, srecv, att,
    loc_sem, a2a_send, a2a_recv, bias_send, bias_recv, q_send, q_recv,
    up_send, dn_send, z_recv, sib_send, sib_recv,
    o_send, o_recv, s_send, s_recv, y_send, y_recv,
):
    z, x, c, y = (lax.axis_index(a) for a in ("z", "x", "c", "head"))
    above, below = (z + 1) % NZ, (z + NZ - 1) % NZ

    def remote(src, dst, send, recv, dz=None, dx=None, dc=None, dy=None):
        return pltpu.make_async_remote_copy(
            src_ref=src, dst_ref=dst, send_sem=send, recv_sem=recv,
            device_id=(
                z if dz is None else dz, x if dx is None else dx,
                c if dc is None else dc, y if dy is None else dy,
            ),
            device_id_type=MESH_ID,
        )

    barrier = pltpu.get_barrier_semaphore()
    peers = [(z, x, c, (y + d) % NY) for d in range(1, NY)]
    peers += [(z, (x + d) % NX, c, y) for d in range(1, NX)]
    peers += [(z, x, 1 - c, y), (above, x, c, y), (below, x, c, y)]
    for peer in peers:
        pl.semaphore_signal(barrier, inc=1, device_id=peer, device_id_type=MESH_ID)
    pl.semaphore_wait(barrier, len(peers))

    own_rows = pl.ds(pl.multiple_of(y * PART, PART), PART)

    def columns(owner):
        return pl.ds(pl.multiple_of(owner * WIDTH, WIDTH), WIDTH)

    landing = [kbuf.at[z, c], vin, qin]
    sources = [k_hbm, v_hbm, q_hbm]

    def token_copy(a, d):
        dest = (y + d) % NY
        return remote(
            sources[a].at[:, columns(dest)], landing[a].at[own_rows, :],
            a2a_send.at[a, d - 1], a2a_recv.at[a, d - 1], dy=dest,
        )

    def own_copy(a):
        return pltpu.make_async_copy(
            sources[a].at[:, columns(y)], landing[a].at[own_rows, :], loc_sem.at[a]
        )

    for a in range(3):
        for d in range(1, NY):
            token_copy(a, d).start()
        own_copy(a).start()

    def bias_copy(d):
        return remote(
            bias_in, bias.at[x], bias_send.at[d - 1], bias_recv.at[d - 1], dx=(x + d) % NX
        )

    for d in range(1, NX):
        bias_copy(d).start()
    bias[x] = bias_in[...]

    def token_wait(a):
        own_copy(a).wait()
        for d in range(1, NY):
            token_copy(a, d).wait_recv()

    bufs = [kbuf, vbuf]

    def block(kv, b, side):
        return bufs[kv].at[b, side]

    def up_copy(kv, b):
        return remote(block(kv, b, c), block(kv, b, c), up_send.at[kv, b], z_recv.at[kv, b], dz=above)

    def down_copy(kv, b):
        return remote(block(kv, b, c), block(kv, b, c), dn_send.at[kv, b], z_recv.at[kv, b], dz=below)

    def side_copy(kv, b, side):
        return remote(
            block(kv, b, side), block(kv, b, side), sib_send.at[kv, b], sib_recv.at[kv, b], dc=1 - c
        )

    def reaches_up(b, plane):
        return (plane < NZ) & ((plane - b <= 3) | (plane == NZ - 1) & (plane - b <= 4))

    def reaches_down(b, plane):
        return (b <= 2) & ((plane >= b + 4) | (plane < b))

    def forward(kv, b, up, down, side):
        @pl.when(side)
        def _():
            side_copy(kv, b, c).start()

        @pl.when(up)
        def _():
            up_copy(kv, b).start()

        @pl.when(down)
        def _():
            down_copy(kv, b).start()

    def finish(kv, b, up, down, side):
        @pl.when(side)
        def _():
            side_copy(kv, b, c).wait_send()

        @pl.when(up)
        def _():
            up_copy(kv, b).wait_send()

        @pl.when(down)
        def _():
            down_copy(kv, b).wait_send()

    own_plan = (z < NZ - 1, z <= 2, z >= 0)

    def rising(step):
        b = z - step
        here = (b >= 0) & reaches_up(jnp.maximum(b, 0), z)
        b = jnp.maximum(b, 0)
        return here, b, (here & reaches_up(b, z + 1), False, here)

    def falling(step):
        b = (z + step) % NZ
        here = reaches_down(b, z)
        return here, b, (False, here & reaches_down(b, below), here & (b < z))

    token_wait(0)
    forward(0, z, *own_plan)
    token_wait(1)
    for h in range(HEADS):
        vbuf[z, c, h * HS : (h + 1) * HS, :] = vin[:, h * HS : (h + 1) * HS].T
    forward(1, z, *own_plan)
    token_wait(2)
    for h in range(HEADS):
        qt[x, h * HS : (h + 1) * HS, :] = qin[:, h * HS : (h + 1) * HS].T

    def query_copy(d):
        return remote(qt.at[x], qt.at[x], q_send.at[d - 1], q_recv.at[d - 1], dx=(x + d) % NX)

    for d in range(1, NX):
        query_copy(d).start()

    acc[...] = jnp.zeros_like(acc)
    top[...] = jnp.full_like(top, NONE)
    total[...] = jnp.zeros_like(total)

    def query_wait(d):
        remote(
            qt.at[(x + NX - d) % NX], qt.at[(x + NX - d) % NX],
            q_send.at[d - 1], q_recv.at[d - 1], dx=(x + d) % NX,
        ).wait_recv()
        behind = bias.at[(x + NX - d) % NX]
        remote(
            behind, behind, bias_send.at[d - 1], bias_recv.at[d - 1], dx=(x + d) % NX
        ).wait_recv()

    def attend(b, r):
        group = b * (NX * NC) + x * NC
        offs = []
        for s in range(NC):
            row = bias[r, pl.ds(group + s, 1), :]
            offs.append(jnp.concatenate([row, row], axis=1))
        for h in range(HEADS):
            span = slice(h * HS, (h + 1) * HS)
            query = qt[r, span, :]
            scores = [
                jnp.dot(kbuf[b, s, :, span], query, preferred_element_type=jnp.float32)
                for s in range(NC)
            ]
            old = top[r, h : h + 1, :]
            new = old
            for s in range(NC):
                new = jnp.maximum(new, jnp.max(scores[s], axis=0, keepdims=True) + offs[s])
            factor = jnp.exp2((old - new) * SCALE)
            weights = [jnp.exp2(scores[s] * SCALE + (offs[s] - new * SCALE)) for s in range(NC)]
            sums = sum(jnp.sum(w, axis=0, keepdims=True) for w in weights)
            total[r, h : h + 1, :] = total[r, h : h + 1, :] * factor + sums
            top[r, h : h + 1, :] = new
            added = sum(
                jnp.dot(
                    vbuf[b, s, span, :], weights[s].astype(jnp.bfloat16),
                    preferred_element_type=jnp.float32,
                )
                for s in range(NC)
            )
            acc[r, span, :] = acc[r, span, :] * factor + added

    def attend_block(b, first):
        if first:
            attend(b, x)
            for d in range(1, NX):
                query_wait(d)
                attend(b, (x + NX - d) % NX)
        else:
            @pl.loop(0, NX)
            def _(r):
                attend(b, r)

    def receive(step):
        for plan in (rising, falling):
            here, b, moves = plan(step)

            @pl.when(here)
            def _():
                for kv in range(2):
                    up_copy(kv, b).wait_recv()
                    forward(kv, b, *moves)

    def side_wait(b):
        for kv in range(2):
            side_copy(kv, b, 1 - c).wait_recv()

    def compute(step):
        for plan in (rising, falling):
            here, b, moves = plan(step)

            @pl.when(moves[2])
            def _():
                side_wait(b)
                attend_block(b, False)

    receive(1)
    side_wait(z)
    attend_block(z, True)

    @pl.loop(2, 5)
    def _(step):
        receive(step)
        compute(step - 1)

    compute(4)

    def result_copy(d):
        return remote(
            osend.at[d - 1], orecv.at[d - 1], o_send.at[d - 1], o_recv.at[d - 1], dx=(x + d) % NX
        )

    def stats_copy(d):
        return remote(
            ssend.at[d - 1], srecv.at[d - 1], s_send.at[d - 1], s_recv.at[d - 1], dx=(x + d) % NX
        )

    for d in range(1, NX):
        r = (x + d) % NX
        ssend[d - 1, 0] = top[r]
        ssend[d - 1, 1] = total[r]
        stats_copy(d).start()
        osend[d - 1] = acc[r].astype(jnp.bfloat16)
        result_copy(d).start()

    for d in range(1, NX):
        stats_copy(d).wait_recv()
        result_copy(d).wait_recv()

    for h in range(HEADS):
        span = slice(h * HS, (h + 1) * HS)
        tops = [top[x, h : h + 1, :]] + [srecv[d, 0, h : h + 1, :] for d in range(NX - 1)]
        totals = [total[x, h : h + 1, :]] + [srecv[d, 1, h : h + 1, :] for d in range(NX - 1)]
        best = functools.reduce(jnp.maximum, tops)
        shares = [jnp.exp2((t - best) * SCALE) for t in tops]
        inverse = 1.0 / sum(s * t for s, t in zip(shares, totals))
        parts = [acc[x, span, :]] + [orecv[d, span, :].astype(jnp.float32) for d in range(NX - 1)]
        merged = sum(p * (s * inverse) for p, s in zip(parts, shares))
        att[:, span] = merged.astype(jnp.bfloat16).T

    def back_copy(d):
        dest = (y + d) % NY
        return remote(
            att.at[pl.ds(pl.multiple_of(dest * PART, PART), PART), :], out_hbm.at[:, columns(y)],
            y_send.at[d - 1], y_recv.at[d - 1], dy=dest,
        )

    keep = pltpu.make_async_copy(att.at[own_rows, :], out_hbm.at[:, columns(y)], loc_sem.at[0])
    for d in range(1, NY):
        back_copy(d).start()
    keep.start()

    for a in range(3):
        for d in range(1, NY):
            token_copy(a, d).wait_send()
    for d in range(1, NX):
        bias_copy(d).wait_send()
        query_copy(d).wait_send()
        result_copy(d).wait_send()
        stats_copy(d).wait_send()
    for kv in range(2):
        finish(kv, z, *own_plan)

    @pl.loop(1, 5)
    def _(step):
        for plan in (rising, falling):
            _, b, moves = plan(step)
            for kv in range(2):
                finish(kv, b, *moves)

    keep.wait()
    for d in range(1, NY):
        back_copy(d).wait()


def attention(query, keys, values, bias):
    dma = pltpu.SemaphoreType.DMA
    bf16, f32 = jnp.bfloat16, jnp.float32
    anywhere = pl.BlockSpec(memory_space=pl.ANY)
    return pl.pallas_call(
        attention_kernel,
        out_shape=jax.ShapeDtypeStruct((PART, NY * WIDTH), bf16),
        in_specs=[anywhere, anywhere, anywhere, pl.BlockSpec(memory_space=pltpu.VMEM)],
        out_specs=anywhere,
        scratch_shapes=[
            pltpu.VMEM((ROWS, WIDTH), bf16),
            pltpu.VMEM((ROWS, WIDTH), bf16),
            pltpu.VMEM((NZ, NC, ROWS, WIDTH), bf16),
            pltpu.VMEM((NZ, NC, WIDTH, ROWS), bf16),
            pltpu.VMEM((NX, WIDTH, ROWS), bf16),
            pltpu.VMEM((NX, GROUPS, HS), f32),
            pltpu.VMEM((NX, WIDTH, ROWS), f32),
            pltpu.VMEM((NX, 8, ROWS), f32),
            pltpu.VMEM((NX, 8, ROWS), f32),
            pltpu.VMEM((NX - 1, WIDTH, ROWS), bf16),
            pltpu.VMEM((NX - 1, WIDTH, ROWS), bf16),
            pltpu.VMEM((NX - 1, 2, 8, ROWS), f32),
            pltpu.VMEM((NX - 1, 2, 8, ROWS), f32),
            pltpu.VMEM((ROWS, WIDTH), bf16),
            dma((3,)), dma((3, NY - 1)), dma((3, NY - 1)),
            dma((NX - 1,)), dma((NX - 1,)), dma((NX - 1,)), dma((NX - 1,)),
            dma((2, NZ)), dma((2, NZ)), dma((2, NZ)), dma((2, NZ)), dma((2, NZ)),
            dma((NX - 1,)), dma((NX - 1,)), dma((NX - 1,)), dma((NX - 1,)),
            dma((NY - 1,)), dma((NY - 1,)),
        ],
        compiler_params=pltpu.CompilerParams(
            collective_id=0, has_side_effects=True, vmem_limit_bytes=40 * 1024 * 1024
        ),
        cost_estimate=pl.CostEstimate(
            flops=192 * 4 * ROWS * ROWS * HS, bytes_accessed=2**22, transcendentals=192 * ROWS * ROWS
        ),
    )(query, keys, values, bias)


def shards(hidden, query, keys, values, attends, levels, out_weight, gate_table):
    half = D // NC
    mine = lax.dynamic_slice_in_dim(out_weight, lax.axis_index("c") * half, half, axis=1)
    gathered = lax.all_gather(mine, ("c", "head"), axis=0, tiled=True)
    gathered = gathered.reshape(NC, NY * WIDTH, half)
    bias = jnp.where(attends[0] > 0, 0.0, NONE).astype(jnp.float32)
    bias = jnp.broadcast_to(bias[:, None], (GROUPS, HS))
    attended = attention(query, keys, values, bias)
    projected = jnp.concatenate(
        [jnp.dot(attended, gathered[s], preferred_element_type=jnp.float32) for s in range(NC)],
        axis=1,
    )
    gate_row = lax.dynamic_index_in_dim(gate_table, levels[0], 0, keepdims=True)
    return (hidden.astype(jnp.float32) + gate_row * projected).astype(jnp.bfloat16)


def solution(mesh):
    fine = Mesh(mesh.devices.reshape(NZ, NX, NC, NY), ("z", "x", "c", "head"))
    tokens = P(("z", "x", "c", "head"), None)
    group = ("z", "x", "c")
    placed = (
        tokens, tokens, tokens, tokens, P(group, None), P(group), P("head", None), P(),
    )
    return jax.shard_map(
        shards, mesh=fine, in_specs=placed, out_specs=tokens, check_vma=False
    )
```

time: 938 us -> 109 us (0.12)
  waiting for transfers between devices: 471 us -> 0.04 us
  starting transfers between devices: 254 us -> 0.01 us
  local copies, waits for them, and re-layouts: 88.6 us -> 6.51 us
  Pallas kernels: 0 us -> 79.8 us
  matrix products: 50.4 us -> 6.57 us
  loops' own time: 40 us -> 0 us
  other arithmetic: 12.8 us -> 1.52 us
    ppermute x126 -> x0, waiting for transfers between devices: 357 us -> none  [from_behind(): return lax.ppermute(block, axis, route)]
    ppermute x126 -> x0, starting transfers between devices: 243 us -> none  [from_behind(): return lax.ppermute(block, axis, route)]
    reduce_scatter x1 -> x0, waiting for transfers between devices: 99.1 us -> none  [shards(): lax.psum_scatter(jnp.dot(attended, out_weight, preferred_element_type=jnp...]
    pallas_call x0 -> x1, Pallas kernels: none -> 79.8 us  [attention(): pl.pallas_call(attention_kernel, out_shape=jax.ShapeDtypeStruct((PART, NY...]
    while x192 -> x0, local copies, waits for them, and re-layouts: 45 us -> none
    dot_general x129 -> x2, matrix products: 50.4 us -> 6.57 us  [shards(): jnp.dot(attended, gathered[s], preferred_element_type=jnp.float32)]
    another operation x1 -> x0, loops' own time: 40 us -> none  [shards(): lax.fori_loop(1, lax.axis_size('group'), chain_step, ((local_keys, local_...]
    dynamic_slice x63 -> x1, local copies, waits for them, and re-layouts: 36.5 us -> 1.08 us  [shards(): lax.dynamic_slice_in_dim(out_weight, lax.axis_index('c') * half, half, ax...]
  transfers between devices with their start and end apart: 130 -> 1, of which waited for: 130 -> 0; matrix products, arithmetic and copies ran while one was open for 8% -> 2% of each run, Pallas kernels for 0% -> 74%
where the time goes in v1:
time: 109 us; the launch traced here: 108 us
  Pallas kernels  79.8 us (73%)
  between operations  14.1 us (13%)
  matrix products  6.57 us (6%)
  local copies, waits for them, and re-layouts  6.51 us (6%)
  other arithmetic  1.52 us (1%)
    pallas_call x1, Pallas kernels, attention(): pl.pallas_call(attention_kernel, out_shape=jax.ShapeDtypeStruct((PART, NY...  79.8 us
    dot_general x2, matrix products, shards(): jnp.dot(attended, gathered[s], preferred_element_type=jnp.float32)  6.57 us
    unnamed x10, local copies, waits for them, and re-layouts  4.45 us
  transfers between devices with their start and end apart: 1, of which 0 were waited for; matrix products, arithmetic and copies ran while one was open for 2% of the time, Pallas kernels for 74%

profile of v1, /device:TPU:224, one launch (start us, length us, event | category | flops | bytes accessed | tf_op | source)
XLA Modules:
  0.0 108.5 jit_solution(14475903346912494611)
XLA Ops:
  6.5 0.0 copy-start
  6.5 0.0 all-gather.2.cloned.1.call-start
  6.5 1.7 %copy-done = bf16[384,3072]{1,0:T(8,128)(2,1)S(1)} copy-done((bf16[384,3072]{1,0:T(8,128)(2,1)S(1)}, bf16[384,3072]{1,0:T(8,128)(2,1)}, u32[]{:S(2)}) %copy-start) | copy-done | bytes 2359320
  8.2 1.1 constant_dynamic-slice_fusion
  9.3 0.0 all-gather.2.cloned.1.call-update
  10.0 0.7 fusion.6
  10.6 0.9 constant_dynamic-slice_fusion.1
  11.5 0.1 broadcast_in_dim.16.bias_in
  11.6 0.0 copy-start.1
  11.6 0.9 copy-done.1
  12.5 0.0 copy-start.2
  12.5 0.9 copy-done.2
  13.5 0.0 copy-start.3
  13.5 0.9 copy-done.3
  14.4 79.8 %shard_map.82 = bf16[64,1536]{1,0:T(8,128)(2,1)S(1)} custom-call(bf16[64,1536]{1,0:T(8,128)(2,1)S(1)} %copy-done.1, bf16[64,1536]{1,0:T(8,128)(2,1)S(1)} %copy-done.2, bf16[64,1536]{1,0:T(8,128)(2,1)S(1)} %copy-done.3, f32[64,128]{1,0:T(8,128)S(1)} %broadcast_in_dim.16.bias_in), custom_call_target="tpu_custom_call" | custom-call | flops 6442450944 | bytes 4194304 | tf_op jit(solution)/shard_map/pallas_call | solution.py:329
  94.1 0.0 copy-start.4
  94.2 0.0 all-gather.2.cloned.1.call-done
  94.2 3.3 %fusion.2 = f32[64,1536]{1,0:T(8,128)S(1)} fusion(bf16[64,1536]{1,0:T(8,128)(2,1)S(1)} %shard_map.82, bf16[3072,1536]{1,0:T(8,128)(2,1)} %all-gather.2.cloned.1.call-done), kind=kOutput, calls=%fused_computation.2 | convolution fusion | flops 301989888 | bytes 5308416 | tf_op jit(solution)/shard_map/dot_general | solution.py:373
  97.5 3.3 %fusion = f32[64,1536]{1,0:T(8,128)S(1)} fusion(bf16[64,1536]{1,0:T(8,128)(2,1)S(1)} %shard_map.82, bf16[3072,1536]{1,0:T(8,128)(2,1)} %all-gather.2.cloned.1.call-done), kind=kOutput, calls=%fused_computation | convolution fusion | flops 301989888 | bytes 5308416 | tf_op jit(solution)/shard_map/dot_general | solution.py:373
  100.8 0.0 copy-done.4
  100.8 0.9 fusion.5
Async XLA Ops:
  6.5 1.7 %copy-start = (bf16[384,3072]{1,0:T(8,128)(2,1)S(1)}, bf16[384,3072]{1,0:T(8,128)(2,1)}, u32[]{:S(2)}) copy-start(bf16[384,3072]{1,0:T(8,128)(2,1)} %param.14) | copy-start | bytes 7077892
  6.5 87.6 %all-gather.2.cloned.1.call-start = ((), (), s32[]{:S(2)}) async-start(), calls=%async_computation | async-start | bytes 10616832 | tf_op jit(solution)/shard_map/all_gather | solution.py:367
  11.6 0.9 copy-start.1
  12.5 0.9 copy-start.2
  13.5 0.9 copy-start.3
  94.1 6.6 %copy-start.4 = (bf16[64,3072]{1,0:T(8,128)(2,1)S(1)}, bf16[64,3072]{1,0:T(8,128)(2,1)}, u32[]{:S(2)}) copy-start(bf16[64,3072]{1,0:T(8,128)(2,1)} %param.8) | copy-start | bytes 1179652
Sparse Core Ops, SparseCore 0:
  9.4 57.6 all-gather.1

commit v2 on v0

v2 whole, which is shorter than its diff:
```python
import functools

import jax
import jax.numpy as jnp
from jax import lax
from jax.experimental import pallas as pl
from jax.experimental.pallas import tpu as pltpu
from jax.sharding import Mesh, PartitionSpec as P

HS = 128
NZ, NX, NC, NY = 8, 4, 2, 4
GROUPS = 64
ROWS = 256
PART = 64
HEADS = 3
D = 3072
HALF = D // NC
TILE = 768
LAST = 4
SCALE = 1.4426950408889634 * HS**-0.5
NONE = -1e30
MESH_ID = pl.DeviceIdType.MESH
F32, BF16 = jnp.float32, jnp.bfloat16


def kernel(
    hidden_hbm, q_hbm, k_hbm, v_hbm, attends_ref, level_ref, w_hbm, gate_hbm, out_ref,
    qin, vin, kbuf, vbuf, qt, bias_out, bias, acc, top, total, osend, orecv, ssend, srecv,
    att, arecv, wbuf, gates, hidden, summed,
    loc_sem, a2a_send, a2a_recv, bias_send, bias_recv, q_send, q_recv,
    up_send, dn_send, z_recv, sib_send, sib_recv,
    o_send, o_recv, s_send, s_recv, y_loc, y_send, y_recv,
    w_loc, w_send, w_recv, far_send, far_recv, wside_send, wside_recv,
):
    z, x, c, y = (lax.axis_index(a) for a in ("z", "x", "c", "head"))
    above, below = (z + 1) % NZ, (z + NZ - 1) % NZ

    def remote(src, dst, send, recv, dz=None, dx=None, dc=None, dy=None):
        return pltpu.make_async_remote_copy(
            src_ref=src, dst_ref=dst, send_sem=send, recv_sem=recv,
            device_id=(
                z if dz is None else dz, x if dx is None else dx,
                c if dc is None else dc, y if dy is None else dy,
            ),
            device_id_type=MESH_ID,
        )

    def span(at, size):
        return pl.ds(pl.multiple_of(at * size, size), size)

    barrier = pltpu.get_barrier_semaphore()
    peers = [(z, x, c, (y + d) % NY) for d in range(1, NY)]
    peers += [(z, (x + d) % NX, c, y) for d in range(1, NX)]
    peers += [(z, x, 1 - c, y), (above, x, c, y), (below, x, c, y)]
    for peer in peers:
        pl.semaphore_signal(barrier, inc=1, device_id=peer, device_id_type=MESH_ID)

    row = attends_ref[...].astype(F32)
    at_row = lax.broadcasted_iota(jnp.int32, (NZ * NC, GROUPS), 0)
    at_column = lax.broadcasted_iota(jnp.int32, (NZ * NC, GROUPS), 1)
    for place in range(NX):
        group = (at_row // NC) * (NX * NC) + place * NC + at_row % NC
        seen = jnp.sum(jnp.where(at_column == group, row, 0.0), axis=1, keepdims=True)
        bias_out[place] = jnp.broadcast_to(jnp.where(seen > 0.5, 0.0, NONE), (NZ * NC, ROWS))
    bias[x] = bias_out[x]

    pl.semaphore_wait(barrier, len(peers))

    sources = [k_hbm, v_hbm, q_hbm]

    def landing(a, h):
        if a == 0:
            return kbuf.at[z, h, pl.ds(pl.multiple_of(c * ROWS + y * PART, PART), PART), :]
        return (vin if a == 1 else qin).at[h, span(y, PART), :]

    def token_copy(a, h, d):
        dest = (y + d) % NY
        return remote(
            sources[a].at[:, span(dest * HEADS + h, HS)], landing(a, h),
            a2a_send.at[a, h, d - 1], a2a_recv.at[a, h, d - 1], dy=dest,
        )

    def own_copy(a, h):
        return pltpu.make_async_copy(
            sources[a].at[:, span(y * HEADS + h, HS)], landing(a, h), loc_sem.at[a, h]
        )

    for h in range(HEADS):
        for a in range(3):
            for d in (2, 1, 3):
                token_copy(a, h, d).start()
            own_copy(a, h).start()

    def bias_copy(d):
        return remote(
            bias_out.at[(x + d) % NX], bias.at[x], bias_send.at[d - 1], bias_recv.at[d - 1],
            dx=(x + d) % NX,
        )

    for d in range(1, NX):
        bias_copy(d).start()

    def token_wait(a, h):
        own_copy(a, h).wait()
        for d in range(1, NY):
            token_copy(a, h, d).wait_recv()

    def block(kv, b, h, side):
        if kv == 0:
            return kbuf.at[b, h, span(side, ROWS), :]
        return vbuf.at[b, h, :, span(side, ROWS)]

    def up_copy(kv, b, h):
        ref = block(kv, b, h, c)
        return remote(ref, ref, up_send.at[kv, b, h], z_recv.at[kv, b, h], dz=above)

    def down_copy(kv, b, h):
        ref = block(kv, b, h, c)
        return remote(ref, ref, dn_send.at[kv, b, h], z_recv.at[kv, b, h], dz=below)

    def side_copy(kv, b, h, side):
        ref = block(kv, b, h, side)
        return remote(ref, ref, sib_send.at[kv, b, h], sib_recv.at[kv, b, h], dc=1 - c)

    def reaches_up(kv, b, plane):
        near = plane - b <= 3
        if kv == 0:
            near = near | ((plane == NZ - 1) & (b == 3))
        return (plane < NZ) & near

    def reaches_down(kv, b, plane):
        there = (b <= 2) & ((plane >= b + 4) | (plane < b))
        if kv == 1:
            there = there | ((b == 3) & ((plane == NZ - 1) | (plane < b)))
        return there

    def when(condition, act):
        @pl.when(condition)
        def _():
            act()

    def each_move(kv, b, h, moves, act):
        up, down, side = moves
        if up is not None:
            when(up, lambda: act(up_copy(kv, b, h)))
        if down is not None:
            when(down, lambda: act(down_copy(kv, b, h)))
        when(side, lambda: act(side_copy(kv, b, h, c)))

    def start(copy):
        copy.start()

    def own_plan(kv):
        return z < NZ - 1, z <= 2 + kv, z >= 0

    def rising(kv, step):
        b = jnp.maximum(z - step, 0)
        here = (z >= step) & reaches_up(kv, b, z)
        return here, b, (here & reaches_up(kv, b, z + 1), None, here)

    def falling(kv, step):
        b = (z + step) % NZ
        here = reaches_down(kv, b, z)
        return here, b, (None, here & reaches_down(kv, b, below), here & (b < z))

    def query_copy(h, d):
        return remote(
            qt.at[h, x], qt.at[h, x], q_send.at[h, d - 1], q_recv.at[h, d - 1], dx=(x + d) % NX
        )

    for h in range(HEADS):
        token_wait(0, h)
        each_move(0, z, h, own_plan(0), start)
        token_wait(1, h)
        vbuf[z, h, :, span(c, ROWS)] = vin[h].T
        each_move(1, z, h, own_plan(1), start)
        token_wait(2, h)
        qt[h, x] = qin[h].T
        for d in (2, 1, 3):
            query_copy(h, d).start()

    def weight_rows(owner, part):
        if part is None:
            return span(owner, HS)
        return pl.ds(pl.multiple_of(owner * HS + part * (HS // 2), HS // 2), HS // 2)

    def weight_ref(h, owner, part, half):
        return wbuf.at[h, weight_rows(owner, part), span(half, HALF)]

    ahead, behind, opposite = (y + 1) % NY, (y + NY - 1) % NY, (y + 2) % NY

    def weight_copy(h, way):
        return remote(
            w_hbm.at[h, :, span(c, HALF)], weight_ref(h, y, None, c),
            w_send.at[h, way], w_recv.at[h, way], dy=(ahead, behind)[way],
        )

    def far_copy(h, way):
        ref = weight_ref(h, (behind, ahead)[way], way, c)
        return remote(
            ref, ref, far_send.at[h, way], far_recv.at[h, way], dy=(ahead, behind)[way]
        )

    def weight_side(h, piece):
        owner, part = ((behind, None), (ahead, None), (opposite, 0), (opposite, 1))[piece]
        ref = weight_ref(h, owner, part, c)
        return remote(ref, ref, wside_send.at[h, piece], wside_recv.at[h, piece], dc=1 - c)

    own_weight = pltpu.make_async_copy(w_hbm, wbuf.at[:, weight_rows(y, None), :], w_loc.at[0])
    gate_copy = pltpu.make_async_copy(gate_hbm, gates, w_loc.at[1])
    hidden_copy = pltpu.make_async_copy(hidden_hbm, hidden, w_loc.at[2])
    for h in range(HEADS):
        for way in range(2):
            weight_copy(h, way).start()
    own_weight.start()
    gate_copy.start()
    hidden_copy.start()

    def weight_near(h):
        for way in range(2):
            weight_copy(h, way).wait_recv()
            far_copy(h, way).start()
            weight_side(h, way).start()

    acc[...] = jnp.zeros_like(acc)
    top[...] = jnp.full_like(top, NONE)
    total[...] = jnp.zeros_like(total)

    def query_wait(h, d):
        ref = qt.at[h, (x + NX - d) % NX]
        remote(ref, ref, q_send.at[h, d - 1], q_recv.at[h, d - 1], dx=(x + d) % NX).wait_recv()

    def bias_wait(d):
        ref = bias.at[(x + NX - d) % NX]
        remote(ref, ref, bias_send.at[d - 1], bias_recv.at[d - 1], dx=(x + d) % NX).wait_recv()

    def attend(blocks, h):
        scores = [
            [jnp.dot(kbuf[b, h], qt[h, r], preferred_element_type=F32) for b in blocks]
            for r in range(NX)
        ]
        for r in range(NX):
            parts, offs = [], []
            for i, b in enumerate(blocks):
                for s in range(NC):
                    parts.append(scores[r][i][s * ROWS : (s + 1) * ROWS])
                    offs.append(bias[r, pl.ds(b * NC + s, 1), :])
            old = top[h, r]
            new = old
            for p, o in zip(parts, offs):
                new = jnp.maximum(new, jnp.max(p, axis=0, keepdims=True) + o)
            factor = jnp.exp2((old - new) * SCALE)
            weights = [jnp.exp2(p * SCALE + (o - new * SCALE)) for p, o in zip(parts, offs)]
            top[h, r] = new
            total[h, r] = total[h, r] * factor + sum(
                jnp.sum(w, axis=0, keepdims=True) for w in weights
            )
            rounded = [w.astype(BF16) for w in weights]
            added = sum(
                jnp.dot(
                    vbuf[b, h], jnp.concatenate(rounded[NC * i : NC * i + NC], axis=0),
                    preferred_element_type=F32,
                )
                for i, b in enumerate(blocks)
            )
            acc[h, r] = acc[h, r] * factor + added

    def arrive(step, h):
        for kv in range(2):
            for plan in (rising, falling):
                here, b, moves = plan(kv, step)

                def take(kv=kv, b=b, moves=moves):
                    up_copy(kv, b, h).wait_recv()
                    each_move(kv, b, h, moves, start)

                when(here, take)

    def side_wait(b, h):
        for kv in range(2):
            side_copy(kv, b, h, 1 - c).wait_recv()

    def result_copy(h, d):
        return remote(
            osend.at[h, d - 1], orecv.at[h, d - 1], o_send.at[h, d - 1], o_recv.at[h, d - 1],
            dx=(x + d) % NX,
        )

    def stats_copy(h, d):
        return remote(
            ssend.at[h, d - 1], srecv.at[h, d - 1], s_send.at[h, d - 1], s_recv.at[h, d - 1],
            dx=(x + d) % NX,
        )

    def hand_over(h):
        for d in (2, 1, 3):
            r = (x + d) % NX
            ssend[h, d - 1, 0:1] = top[h, r]
            ssend[h, d - 1, 1:2] = total[h, r]
            stats_copy(h, d).start()
            osend[h, d - 1] = acc[h, r].astype(BF16)
            result_copy(h, d).start()

    @pl.loop(0, (LAST + 1) * HEADS)
    def _(i):
        step, h = i // HEADS, i % HEADS

        @pl.when(step < LAST - 1)
        def _():
            arrive(step + 1, h)

        @pl.when(step == LAST)
        def _():
            arrive(step, h)

        @pl.when(step == 0)
        def _():
            for d in range(1, NX):
                query_wait(h, d)

        @pl.when(i == 0)
        def _():
            for d in range(1, NX):
                bias_wait(d)

        low = jnp.maximum(z - step, 0)
        high = (z + step) % NZ
        has_low = (z >= step) & reaches_up(0, low, z)
        has_high = (step > 0) & reaches_down(0, high, z) & (high < z)
        when(has_low, lambda: side_wait(low, h))
        when(has_high, lambda: side_wait(high, h))
        when(has_low & has_high, lambda: attend([low, high], h))
        when(
            has_low != has_high,
            lambda: attend([jnp.where(has_low, low, high)], h),
        )

        for at, piece in ((4, 0), (7, 1), (11, 2)):
            when(i == at, lambda piece=piece: weight_near(piece))

        when(step == LAST, lambda: hand_over(h))

    def back_copy(h, d):
        dest = (y + d) % NY
        return remote(
            att.at[h, span(dest, PART), :], arecv.at[h, :, span(y, HS)],
            y_send.at[h, d - 1], y_recv.at[h, d - 1], dy=dest,
        )

    def keep_copy(h):
        return pltpu.make_async_copy(
            att.at[h, span(y, PART), :], arecv.at[h, :, span(y, HS)], y_loc.at[h]
        )

    for h in range(HEADS):
        for d in range(1, NX):
            stats_copy(h, d).wait_recv()
            result_copy(h, d).wait_recv()
        tops = [top[h, x]] + [srecv[h, d, 0:1] for d in range(NX - 1)]
        totals = [total[h, x]] + [srecv[h, d, 1:2] for d in range(NX - 1)]
        best = functools.reduce(jnp.maximum, tops)
        shares = [jnp.exp2((t - best) * SCALE) for t in tops]
        inverse = 1.0 / sum(s * t for s, t in zip(shares, totals))
        parts = [acc[h, x]] + [orecv[h, d].astype(F32) for d in range(NX - 1)]
        merged = sum(p * (s * inverse) for p, s in zip(parts, shares))
        att[h] = merged.astype(BF16).T
        for d in (2, 1, 3):
            back_copy(h, d).start()
        keep_copy(h).start()

    gate_copy.wait()
    hidden_copy.wait()
    own_weight.wait()
    for h in range(HEADS):
        for way in range(2):
            far_copy(h, way).wait_recv()
            weight_side(h, 2 + way).start()
        for piece in range(2):
            weight_side(h, piece).wait_recv()
        keep_copy(h).wait()
        for d in range(1, NY):
            back_copy(h, d).wait_recv()
        for piece in range(2, 4):
            weight_side(h, piece).wait_recv()

        @pl.loop(0, D // TILE)
        def _(j, h=h):
            columns = span(j, TILE)
            part = jnp.dot(arecv[h], wbuf[h, :, columns], preferred_element_type=F32)
            if h > 0:
                part = part + summed[:, columns]
            if h < HEADS - 1:
                summed[:, columns] = part
            else:
                gated = gates[pl.ds(level_ref[0], 1), columns] * part
                out_ref[:, columns] = (hidden[:, columns].astype(F32) + gated).astype(BF16)

    def ended(copy):
        copy.wait_send()

    for h in range(HEADS):
        for d in range(1, NY):
            for a in range(3):
                token_copy(a, h, d).wait_send()
            query_copy(h, d).wait_send()
            result_copy(h, d).wait_send()
            stats_copy(h, d).wait_send()
            back_copy(h, d).wait_send()
        for way in range(2):
            weight_copy(h, way).wait_send()
            far_copy(h, way).wait_send()
        for piece in range(4):
            weight_side(h, piece).wait_send()
        for kv in range(2):
            each_move(kv, z, h, own_plan(kv), ended)
    for d in range(1, NX):
        bias_copy(d).wait_send()

    @pl.loop(HEADS, (LAST + 1) * HEADS)
    def _(i):
        step, h = i // HEADS, i % HEADS
        for kv in range(2):
            for plan in (rising, falling):
                _, b, moves = plan(kv, step)
                each_move(kv, b, h, moves, ended)


def fused(hidden, query, keys, values, attends, levels, weight, gate_table):
    dma = pltpu.SemaphoreType.DMA
    vmem = pltpu.VMEM
    hbm = pl.BlockSpec(memory_space=pltpu.HBM)
    local = pl.BlockSpec(memory_space=pltpu.VMEM)
    others = (HEADS, NX - 1)
    moving = (2, NZ, HEADS)
    return pl.pallas_call(
        kernel,
        out_shape=jax.ShapeDtypeStruct((PART, D), BF16),
        in_specs=[
            hbm, hbm, hbm, hbm, local, pl.BlockSpec(memory_space=pltpu.SMEM), hbm, hbm,
        ],
        out_specs=local,
        scratch_shapes=[
            vmem((HEADS, ROWS, HS), BF16),
            vmem((HEADS, ROWS, HS), BF16),
            vmem((NZ, HEADS, NC * ROWS, HS), BF16),
            vmem((NZ, HEADS, HS, NC * ROWS), BF16),
            vmem((HEADS, NX, HS, ROWS), BF16),
            vmem((NX, NZ * NC, ROWS), F32),
            vmem((NX, NZ * NC, ROWS), F32),
            vmem((HEADS, NX, HS, ROWS), F32),
            vmem((HEADS, NX, 1, ROWS), F32),
            vmem((HEADS, NX, 1, ROWS), F32),
            vmem((HEADS, NX - 1, HS, ROWS), BF16),
            vmem((HEADS, NX - 1, HS, ROWS), BF16),
            vmem((HEADS, NX - 1, 2, ROWS), F32),
            vmem((HEADS, NX - 1, 2, ROWS), F32),
            vmem((HEADS, ROWS, HS), BF16),
            vmem((HEADS, PART, NY * HS), BF16),
            vmem((HEADS, NY * HS, D), BF16),
            vmem((GROUPS, D), F32),
            vmem((PART, D), BF16),
            vmem((PART, D), F32),
            dma((3, HEADS)), dma((3, HEADS, NY - 1)), dma((3, HEADS, NY - 1)),
            dma((NX - 1,)), dma((NX - 1,)), dma(others), dma(others),
            dma(moving), dma(moving), dma(moving), dma(moving), dma(moving),
            dma(others), dma(others), dma(others), dma(others),
            dma((HEADS,)), dma(others), dma(others),
            dma((3,)), dma((HEADS, 2)), dma((HEADS, 2)), dma((HEADS, 2)), dma((HEADS, 2)),
            dma((HEADS, 4)), dma((HEADS, 4)),
        ],
        compiler_params=pltpu.CompilerParams(
            collective_id=0, has_side_effects=True, vmem_limit_bytes=48 * 1024 * 1024
        ),
    )(hidden, query, keys, values, attends, levels, weight, gate_table)


def shards(hidden, query, keys, values, attends, levels, out_weight, gate_table):
    weight = out_weight.reshape(HEADS, HS, D)
    return fused(hidden, query, keys, values, attends, levels, weight, gate_table)


def solution(mesh):
    fine = Mesh(mesh.devices.reshape(NZ, NX, NC, NY), ("z", "x", "c", "head"))
    tokens = P(("z", "x", "c", "head"), None)
    group = ("z", "x", "c")
    placed = (
        tokens, tokens, tokens, tokens, P(group, None), P(group), P("head", None), P(),
    )
    return jax.shard_map(
        shards, mesh=fine, in_specs=placed, out_specs=tokens, check_vma=False
    )
```

time: 938 us -> 79.1 us (0.08)
  waiting for transfers between devices: 471 us -> 0 us
  starting transfers between devices: 254 us -> 0 us
  local copies, waits for them, and re-layouts: 88.6 us -> 7.97 us
  Pallas kernels: 0 us -> 69.9 us
  matrix products: 50.4 us -> 0 us
  loops' own time: 40 us -> 0 us
  between operations: 14.2 us -> 0.67 us
  other arithmetic: 12.8 us -> 0 us
    ppermute x126 -> x0, waiting for transfers between devices: 357 us -> none  [from_behind(): return lax.ppermute(block, axis, route)]
    ppermute x126 -> x0, starting transfers between devices: 243 us -> none  [from_behind(): return lax.ppermute(block, axis, route)]
    reduce_scatter x1 -> x0, waiting for transfers between devices: 99.1 us -> none  [shards(): lax.psum_scatter(jnp.dot(attended, out_weight, preferred_element_type=jnp...]
    pallas_call x0 -> x1, Pallas kernels: none -> 69.9 us  [fused(): pl.pallas_call(kernel, out_shape=jax.ShapeDtypeStruct((PART, D), BF16), i...]
    dot_general x129 -> x0, matrix products: 50.4 us -> none  [the longest x64 27.6 us: absorb(): jnp.einsum('hqk,khd->hqd', weights.astype(jnp.bfloat16), value_three, pre...]
    while x192 -> x0, local copies, waits for them, and re-layouts: 45 us -> none
    another operation x1 -> x0, loops' own time: 40 us -> none  [shards(): lax.fori_loop(1, lax.axis_size('group'), chain_step, ((local_keys, local_...]
    dynamic_slice x64 -> x0, local copies, waits for them, and re-layouts: 37.4 us -> none  [the longest x63 36.5 us: chain_step(): lax.dynamic_index_in_dim(attend_row, clipped, 0, keepdims=False) > 0]
  transfers between devices with their start and end apart: 130 -> 0, of which waited for: 130 -> 0; matrix products, arithmetic and copies ran while one was open for 8% -> 0% of each run, Pallas kernels for 0% -> 0%
where the time goes in v2:
time: 79.1 us; the launch traced here: 78.5 us
  Pallas kernels  69.9 us (88%)
  local copies, waits for them, and re-layouts  7.97 us (10%)
    pallas_call x1, Pallas kernels, fused(): pl.pallas_call(kernel, out_shape=jax.ShapeDtypeStruct((PART, D), BF16), i...  69.9 us
    unnamed x15, local copies, waits for them, and re-layouts  7.97 us

profile of v2, /device:TPU:224, one launch (start us, length us, event | category | flops | bytes accessed | tf_op | source)
XLA Modules:
  0.0 78.5 jit_solution(7180249380218728498)
XLA Ops:
  0.7 0.0 copy-start
  0.7 1.7 %copy-done = bf16[384,3072]{1,0:T(8,128)(2,1)S(1)} copy-done((bf16[384,3072]{1,0:T(8,128)(2,1)S(1)}, bf16[384,3072]{1,0:T(8,128)(2,1)}, u32[]{:S(2)}) %copy-start) | copy-done | bytes 2359320
  2.3 0.0 copy-start.1
  2.3 1.1 %copy-done.1 = f32[64,3072]{1,0:T(8,128)S(1)} copy-done((f32[64,3072]{1,0:T(8,128)S(1)}, f32[64,3072]{1,0:T(8,128)}, u32[]{:S(2)}) %copy-start.1) | copy-done | bytes 786456
  3.5 0.0 copy-start.2
  3.5 1.0 %copy-done.2 = bf16[64,3072]{1,0:T(8,128)(2,1)S(1)} copy-done((bf16[64,3072]{1,0:T(8,128)(2,1)S(1)}, bf16[64,3072]{1,0:T(8,128)(2,1)}, u32[]{:S(2)}) %copy-start.2) | copy-done | bytes 393240
  4.4 0.0 copy-start.3
  4.5 0.9 %copy-done.3 = bf16[64,1536]{1,0:T(8,128)(2,1)S(1)} copy-done((bf16[64,1536]{1,0:T(8,128)(2,1)S(1)}, bf16[64,1536]{1,0:T(8,128)(2,1)}, u32[]{:S(2)}) %copy-start.3) | copy-done | bytes 196632
  5.4 0.0 copy-start.4
  5.4 0.9 %copy-done.4 = bf16[64,1536]{1,0:T(8,128)(2,1)S(1)} copy-done((bf16[64,1536]{1,0:T(8,128)(2,1)S(1)}, bf16[64,1536]{1,0:T(8,128)(2,1)}, u32[]{:S(2)}) %copy-start.4) | copy-done | bytes 196632
  6.3 0.0 copy-start.5
  6.3 0.9 %copy-done.5 = bf16[64,1536]{1,0:T(8,128)(2,1)S(1)} copy-done((bf16[64,1536]{1,0:T(8,128)(2,1)S(1)}, bf16[64,1536]{1,0:T(8,128)(2,1)}, u32[]{:S(2)}) %copy-start.5) | copy-done | bytes 196632
  7.2 0.0 copy-start.6
  7.2 0.7 copy-done.6
  7.9 69.9 %shard_map.82 = bf16[64,3072]{1,0:T(8,128)(2,1)S(1)} custom-call(bf16[64,3072]{1,0:T(8,128)(2,1)S(1)} %copy-done.2, bf16[64,1536]{1,0:T(8,128)(2,1)S(1)} %copy-done.3, bf16[64,1536]{1,0:T(8,128)(2,1)S(1)} %copy-done.4, bf16[64,1536]{1,0:T(8,128)(2,1)S(1)} %copy-done.5, s32[1,64]{1,0:T(1,128)S(1)} %copy-done.6, s32[1]{0:T(128)S(6)} %copy.10.level_ref, ...), custom_call_target="tpu_custom_call" | custom-call | tf_op jit(solution)/shard_map/pallas_call | solution.py:435
  77.8 0.7 copy.11
Async XLA Ops:
  0.7 1.7 %copy-start = (bf16[384,3072]{1,0:T(8,128)(2,1)S(1)}, bf16[384,3072]{1,0:T(8,128)(2,1)}, u32[]{:S(2)}) copy-start(bf16[384,3072]{1,0:T(8,128)(2,1)} %param.14) | copy-start | bytes 7077892
  2.3 1.1 %copy-start.1 = (f32[64,3072]{1,0:T(8,128)S(1)}, f32[64,3072]{1,0:T(8,128)}, u32[]{:S(2)}) copy-start(f32[64,3072]{1,0:T(8,128)} %gate_hbm.1) | copy-start | bytes 2359300
  3.5 1.0 %copy-start.2 = (bf16[64,3072]{1,0:T(8,128)(2,1)S(1)}, bf16[64,3072]{1,0:T(8,128)(2,1)}, u32[]{:S(2)}) copy-start(bf16[64,3072]{1,0:T(8,128)(2,1)} %hidden_hbm.1) | copy-start | bytes 1179652
  4.4 0.9 %copy-start.3 = (bf16[64,1536]{1,0:T(8,128)(2,1)S(1)}, bf16[64,1536]{1,0:T(8,128)(2,1)}, u32[]{:S(2)}) copy-start(bf16[64,1536]{1,0:T(8,128)(2,1)} %q_hbm.1) | copy-start | bytes 589828
  5.4 0.9 %copy-start.4 = (bf16[64,1536]{1,0:T(8,128)(2,1)S(1)}, bf16[64,1536]{1,0:T(8,128)(2,1)}, u32[]{:S(2)}) copy-start(bf16[64,1536]{1,0:T(8,128)(2,1)} %k_hbm.1) | copy-start | bytes 589828
  6.3 0.9 %copy-start.5 = (bf16[64,1536]{1,0:T(8,128)(2,1)S(1)}, bf16[64,1536]{1,0:T(8,128)(2,1)}, u32[]{:S(2)}) copy-start(bf16[64,1536]{1,0:T(8,128)(2,1)} %v_hbm.1) | copy-start | bytes 589828
  7.2 0.7 copy-start.6

commit v3 on v0

v3 whole, which is shorter than its diff:
```python
import functools

import jax
import jax.numpy as jnp
from jax import lax
from jax.experimental import pallas as pl
from jax.experimental.pallas import tpu as pltpu
from jax.sharding import Mesh, PartitionSpec as P

HS = 128
NZ, NX, NC, NY = 8, 4, 2, 4
GROUPS = 64
ROWS = 256
PART = 64
HEADS = 3
D = 3072
HALF = D // NC
TILE = 768
LAST = 4
SCALE = 1.4426950408889634 * HS**-0.5
NONE = -1e30
MESH_ID = pl.DeviceIdType.MESH
F32, BF16 = jnp.float32, jnp.bfloat16


def kernel(
    hidden_hbm, q_hbm, k_hbm, v_hbm, attends_hbm, level_ref, w_hbm, gate_hbm, out_hbm,
    attends, qin, kvin, kv, qt, bias_out, bias, acc, top, total, osend, orecv, ssend, srecv,
    att, arecv, wbuf, gates, hidden, summed, out,
    early_sem, token_send, kv_sem, q_sem, bias_send, bias_recv, q_send, q_recv,
    up_send, dn_send, z_recv, sib_send, sib_recv,
    o_send, o_recv, s_send, s_recv, y_send, y_recv,
    w_send, w_recv, far_send, far_recv, near_send, near_recv, side_send, side_recv, out_sem,
):
    z, x, c, y = (lax.axis_index(a) for a in ("z", "x", "c", "head"))
    above, below = (z + 1) % NZ, (z + NZ - 1) % NZ

    def remote(src, dst, send, recv, dz=None, dx=None, dc=None, dy=None):
        return pltpu.make_async_remote_copy(
            src_ref=src, dst_ref=dst, send_sem=send, recv_sem=recv,
            device_id=(
                z if dz is None else dz, x if dx is None else dx,
                c if dc is None else dc, y if dy is None else dy,
            ),
            device_id_type=MESH_ID,
        )

    def span(at, size):
        return pl.ds(pl.multiple_of(at * size, size), size)

    def wait_bytes(ref, sem):
        pltpu.make_async_copy(ref, ref, sem).wait()

    attends_copy = pltpu.make_async_copy(attends_hbm, attends, early_sem.at[0])
    own_weight = pltpu.make_async_copy(w_hbm, wbuf.at[:, span(y, HS), :], early_sem.at[1])
    gate_copy = pltpu.make_async_copy(gate_hbm, gates, early_sem.at[2])
    hidden_copy = pltpu.make_async_copy(hidden_hbm, hidden, early_sem.at[3])
    attends_copy.start()

    barrier = pltpu.get_barrier_semaphore()
    peers = [(z, x, c, (y + d) % NY) for d in range(1, NY)]
    peers += [(z, (x + d) % NX, c, y) for d in range(1, NX)]
    peers += [(z, x, 1 - c, y), (above, x, c, y), (below, x, c, y)]
    for peer in peers:
        pl.semaphore_signal(barrier, inc=1, device_id=peer, device_id_type=MESH_ID)
    pl.semaphore_wait(barrier, len(peers))

    sources = [k_hbm, v_hbm, q_hbm]

    def landing(a, h):
        return (kvin.at[h, a] if a < 2 else qin.at[h]).at[span(y, PART), :]

    def landed(a, h):
        return (kv_sem if a < 2 else q_sem).at[h]

    def token_copy(a, h, d):
        dest = (y + d) % NY
        return remote(
            sources[a].at[:, span(dest * HEADS + h, HS)], landing(a, h),
            token_send.at[a], landed(a, h), dy=dest,
        )

    for h in range(HEADS):
        for a in range(3):
            for d in (2, 1, 3):
                token_copy(a, h, d).start()
            pltpu.make_async_copy(
                sources[a].at[:, span(y * HEADS + h, HS)], landing(a, h), landed(a, h)
            ).start()

    def up_copy(b, h):
        ref = kv.at[b, h, c]
        return remote(ref, ref, up_send.at[b, h], z_recv.at[b, h], dz=above)

    def down_copy(b, h):
        ref = kv.at[b, h, c]
        return remote(ref, ref, dn_send.at[b, h], z_recv.at[b, h], dz=below)

    def side_copy(b, h, side):
        ref = kv.at[b, h, side]
        return remote(ref, ref, sib_send.at[b, h], sib_recv.at[b, h], dc=1 - c)

    def reaches_up(b, h, plane):
        return (plane < NZ) & ((plane - b <= 3) | ((plane == NZ - 1) & (b == 3) & (h < 2)))

    def reaches_down(b, h, plane):
        return ((b <= 2) & ((plane >= b + 4) | (plane < b))) | (
            (b == 3) & (h == 2) & ((plane == NZ - 1) | (plane < b))
        )

    def when(condition, act):
        @pl.when(condition)
        def _():
            act()

    def each_move(b, h, moves, act):
        up, down, side = moves
        if up is not None:
            when(up, lambda: act(up_copy(b, h)))
        if down is not None:
            when(down, lambda: act(down_copy(b, h)))
        when(side, lambda: act(side_copy(b, h, c)))

    def start(copy):
        copy.start()

    def ended(copy):
        copy.wait_send()

    def own_plan(h):
        return z < NZ - 1, z <= (3 if h == 2 else 2), z >= 0

    def rising(step, h):
        b = jnp.maximum(z - step, 0)
        here = (z >= step) & reaches_up(b, h, z)
        return here, b, (here & reaches_up(b, h, z + 1), None, here)

    def falling(step, h):
        b = (z + step) % NZ
        here = reaches_down(b, h, z)
        return here, b, (None, here & reaches_down(b, h, below), here & (b < z))

    def query_copy(h, d):
        return remote(qt.at[h, x], qt.at[h, x], q_send.at[h], q_recv.at[h], dx=(x + d) % NX)

    ahead, behind, opposite = (y + 1) % NY, (y + NY - 1) % NY, (y + 2) % NY

    def weight_ref(h, owner, part):
        rows = span(owner, HS) if part is None else span(owner * 2 + part, HS // 2)
        return wbuf.at[h, rows, span(c, HALF)]

    def weight_bytes(h, rows):
        return wbuf.at[h, 0:rows, 0:HALF]

    def weight_copy(h, way):
        return remote(
            w_hbm.at[h, :, span(c, HALF)], weight_ref(h, y, None),
            w_send.at[h], w_recv.at[h], dy=(ahead, behind)[way],
        )

    def far_copy(h, way):
        ref = weight_ref(h, (behind, ahead)[way], way)
        return remote(ref, ref, far_send.at[h], far_recv.at[h], dy=(ahead, behind)[way])

    def near_side(h, way):
        ref = weight_ref(h, (behind, ahead)[way], None)
        return remote(ref, ref, near_send.at[h], near_recv.at[h], dc=1 - c)

    def far_side(h, way):
        ref = weight_ref(h, opposite, way)
        return remote(ref, ref, side_send.at[h], side_recv.at[h], dc=1 - c)

    def weight_start(h):
        for way in range(2):
            weight_copy(h, way).start()

    def weight_near(h):
        wait_bytes(weight_bytes(h, 2 * HS), w_recv.at[h])
        for way in range(2):
            far_copy(h, way).start()
        for way in range(2):
            near_side(h, way).start()

    def weight_far(h):
        wait_bytes(weight_bytes(h, HS), far_recv.at[h])
        for way in range(2):
            far_side(h, way).start()

    for h in range(HEADS):
        wait_bytes(kvin.at[h], kv_sem.at[h])
        kv[z, h, c, 0:ROWS, :] = kvin[h, 0]
        turned = kvin[h, 1].T
        kv[z, h, c, ROWS : ROWS + HS, :] = turned[:, :HS]
        kv[z, h, c, ROWS + HS :, :] = turned[:, HS:]
        each_move(z, h, own_plan(h), start)
        wait_bytes(qin.at[h], q_sem.at[h])
        qt[h, x] = qin[h].T
        for d in (2, 1, 3):
            query_copy(h, d).start()
        weight_start(h)

    attends_copy.wait()
    row = attends[...].astype(F32)
    at_row = lax.broadcasted_iota(jnp.int32, (NZ * NC, GROUPS), 0)
    at_column = lax.broadcasted_iota(jnp.int32, (NZ * NC, GROUPS), 1)
    for place in range(NX):
        group = (at_row // NC) * (NX * NC) + place * NC + at_row % NC
        seen = jnp.sum(jnp.where(at_column == group, row, 0.0), axis=1, keepdims=True)
        bias_out[place] = jnp.broadcast_to(jnp.where(seen > 0.5, 0.0, NONE), (NZ * NC, ROWS))
    bias[x] = bias_out[x]

    def bias_copy(d):
        return remote(bias_out.at[(x + d) % NX], bias.at[x], bias_send, bias_recv, dx=(x + d) % NX)

    for d in range(1, NX):
        bias_copy(d).start()
    own_weight.start()
    gate_copy.start()
    hidden_copy.start()
    acc[...] = jnp.zeros_like(acc)
    top[...] = jnp.full_like(top, NONE)
    total[...] = jnp.zeros_like(total)

    def attend(blocks, h):
        keys = [jnp.concatenate([kv[b, h, s, :ROWS] for s in range(NC)], axis=0) for b in blocks]
        values = [
            jnp.concatenate(
                [kv[b, h, s, ROWS + i * HS : ROWS + i * HS + HS] for s in range(NC) for i in (0, 1)],
                axis=1,
            )
            for b in blocks
        ]
        scores = [
            [jnp.dot(k, qt[h, r], preferred_element_type=F32) for k in keys] for r in range(NX)
        ]
        for r in range(NX):
            parts, offs = [], []
            for i, b in enumerate(blocks):
                for s in range(NC):
                    parts.append(scores[r][i][s * ROWS : (s + 1) * ROWS])
                    offs.append(bias[r, pl.ds(b * NC + s, 1), :])
            old = top[h, r]
            new = old
            for p, o in zip(parts, offs):
                new = jnp.maximum(new, jnp.max(p, axis=0, keepdims=True) + o)
            factor = jnp.exp2((old - new) * SCALE)
            weights = [jnp.exp2(p * SCALE + (o - new * SCALE)) for p, o in zip(parts, offs)]
            top[h, r] = new
            total[h, r] = total[h, r] * factor + sum(
                jnp.sum(w, axis=0, keepdims=True) for w in weights
            )
            rounded = [w.astype(BF16) for w in weights]
            added = sum(
                jnp.dot(
                    v, jnp.concatenate(rounded[NC * i : NC * i + NC], axis=0),
                    preferred_element_type=F32,
                )
                for i, v in enumerate(values)
            )
            acc[h, r] = acc[h, r] * factor + added

    def arrive(step, h):
        for plan in (rising, falling):
            here, b, moves = plan(step, h)

            def take(b=b, moves=moves):
                up_copy(b, h).wait_recv()
                each_move(b, h, moves, start)

            when(here, take)

    def result_copy(h, d):
        return remote(
            osend.at[h, d - 1], orecv.at[h, d - 1], o_send.at[h], o_recv.at[h], dx=(x + d) % NX
        )

    def stats_copy(h, d):
        return remote(
            ssend.at[h, d - 1], srecv.at[h, d - 1], s_send.at[h], s_recv.at[h], dx=(x + d) % NX
        )

    def hand_over(h):
        for d in (2, 1, 3):
            r = (x + d) % NX
            ssend[h, d - 1, 0:1] = top[h, r]
            ssend[h, d - 1, 1:2] = total[h, r]
            stats_copy(h, d).start()
            osend[h, d - 1] = acc[h, r].astype(BF16)
            result_copy(h, d).start()

    def back_copy(h, d):
        dest = (y + d) % NY
        return remote(
            att.at[h, span(dest, PART), :], arecv.at[h, :, span(y, HS)],
            y_send.at[h], y_recv.at[h], dy=dest,
        )

    def merge(h):
        wait_bytes(srecv.at[h], s_recv.at[h])
        wait_bytes(orecv.at[h], o_recv.at[h])
        tops = [top[h, x]] + [srecv[h, d, 0:1] for d in range(NX - 1)]
        totals = [total[h, x]] + [srecv[h, d, 1:2] for d in range(NX - 1)]
        best = functools.reduce(jnp.maximum, tops)
        shares = [jnp.exp2((t - best) * SCALE) for t in tops]
        inverse = 1.0 / sum(s * t for s, t in zip(shares, totals))
        parts = [acc[h, x]] + [orecv[h, d].astype(F32) for d in range(NX - 1)]
        merged = sum(p * (s * inverse) for p, s in zip(parts, shares))
        att[h] = merged.astype(BF16).T
        for d in (2, 1, 3):
            back_copy(h, d).start()
        pltpu.make_async_copy(
            att.at[h, span(y, PART), :], arecv.at[h, :, span(y, HS)], y_recv.at[h]
        ).start()

    def settle(h):
        wait_bytes(qt.at[h, 0 : NX - 1], q_send.at[h])
        each_move(z, h, (z < NZ - 1, (z <= 2) | ((z == 3) & (h == 2)), z >= 0), ended)

        @pl.loop(1, LAST + 1)
        def _(step):
            for plan in (rising, falling):
                _, b, moves = plan(step, h)
                each_move(b, h, moves, ended)

    @pl.loop(0, (LAST + 1) * HEADS + 1)
    def _(i):
        step, h = i // HEADS, i % HEADS

        when(step < LAST - 1, lambda: arrive(step + 1, h))
        when(step == LAST, lambda: arrive(step, h))
        when(step == 0, lambda: wait_bytes(qt.at[h, 0 : NX - 1], q_recv.at[h]))
        when(i == 0, lambda: wait_bytes(bias.at[0 : NX - 1], bias_recv))

        low = jnp.maximum(z - step, 0)
        high = (z + step) % NZ
        has_low = (step <= LAST) & (z >= step) & reaches_up(low, h, z)
        has_high = (step > 0) & (step <= LAST) & reaches_down(high, h, z) & (high < z)
        when(has_low, lambda: side_copy(low, h, 1 - c).wait_recv())
        when(has_high, lambda: side_copy(high, h, 1 - c).wait_recv())
        when(has_low & has_high, lambda: attend([low, high], h))
        when(has_low != has_high, lambda: attend([jnp.where(has_low, low, high)], h))

        for at, piece in ((4, 0), (7, 1), (11, 2)):
            when(i == at, lambda piece=piece: weight_near(piece))

        @pl.when(step == LAST)
        def _():
            hand_over(h)
            settle(h)

        when(i > LAST * HEADS, lambda: merge((i - 1) % HEADS))

    weight_far(0)
    for a in range(3):
        wait_bytes(sources[a].at[:, 0 : 3 * HEADS * HS], token_send.at[a])
    wait_bytes(bias.at[0 : NX - 1], bias_send)
    gate_copy.wait()
    hidden_copy.wait()
    own_weight.wait()

    def out_copy(j):
        columns = pl.ds(j * TILE, TILE)
        return pltpu.make_async_copy(out.at[:, columns], out_hbm.at[:, columns], out_sem.at[j])

    for h in range(HEADS):
        if h > 0:
            weight_far(h)
        wait_bytes(weight_bytes(h, 2 * HS), near_recv.at[h])
        wait_bytes(arecv.at[h], y_recv.at[h])
        wait_bytes(weight_bytes(h, HS), side_recv.at[h])
        for j in range(D // TILE):
            columns = slice(j * TILE, (j + 1) * TILE)
            part = jnp.dot(arecv[h], wbuf[h, :, columns], preferred_element_type=F32)
            if h > 0:
                part = part + summed[:, columns]
            if h < HEADS - 1:
                summed[:, columns] = part
            else:
                gated = gates[pl.ds(level_ref[0], 1), columns] * part
                out[:, columns] = (hidden[:, columns].astype(F32) + gated).astype(BF16)
                out_copy(j).start()

    for h in range(HEADS):
        wait_bytes(osend.at[h], o_send.at[h])
        wait_bytes(ssend.at[h], s_send.at[h])
        wait_bytes(att.at[h, 0 : 3 * PART], y_send.at[h])
        wait_bytes(weight_bytes(h, 2 * HS), w_send.at[h])
        wait_bytes(weight_bytes(h, HS), far_send.at[h])
        wait_bytes(weight_bytes(h, 2 * HS), near_send.at[h])
        wait_bytes(weight_bytes(h, HS), side_send.at[h])
    for j in range(D // TILE):
        out_copy(j).wait()


def fused(hidden, query, keys, values, attends, levels, weight, gate_table):
    dma = pltpu.SemaphoreType.DMA
    vmem = pltpu.VMEM
    hbm = pl.BlockSpec(memory_space=pltpu.HBM)
    each = dma((HEADS,))
    moving = dma((NZ, HEADS))
    return pl.pallas_call(
        kernel,
        out_shape=jax.ShapeDtypeStruct((PART, D), BF16),
        in_specs=[hbm, hbm, hbm, hbm, hbm, pl.BlockSpec(memory_space=pltpu.SMEM), hbm, hbm],
        out_specs=hbm,
        scratch_shapes=[
            vmem((1, GROUPS), jnp.int32),
            vmem((HEADS, ROWS, HS), BF16),
            vmem((HEADS, 2, ROWS, HS), BF16),
            vmem((NZ, HEADS, NC, 2 * ROWS, HS), BF16),
            vmem((HEADS, NX, HS, ROWS), BF16),
            vmem((NX, NZ * NC, ROWS), F32),
            vmem((NX, NZ * NC, ROWS), F32),
            vmem((HEADS, NX, HS, ROWS), F32),
            vmem((HEADS, NX, 1, ROWS), F32),
            vmem((HEADS, NX, 1, ROWS), F32),
            vmem((HEADS, NX - 1, HS, ROWS), BF16),
            vmem((HEADS, NX - 1, HS, ROWS), BF16),
            vmem((HEADS, NX - 1, 2, ROWS), F32),
            vmem((HEADS, NX - 1, 2, ROWS), F32),
            vmem((HEADS, ROWS, HS), BF16),
            vmem((HEADS, PART, NY * HS), BF16),
            vmem((HEADS, NY * HS, D), BF16),
            vmem((GROUPS, D), F32),
            vmem((PART, D), BF16),
            vmem((PART, D), F32),
            vmem((PART, D), BF16),
            dma((4,)), dma((3,)), each, each, dma(()), dma(()), each, each,
            moving, moving, moving, moving, moving,
            each, each, each, each, each, each,
            each, each, each, each, each, each, each, each, dma((D // TILE,)),
        ],
        compiler_params=pltpu.CompilerParams(
            collective_id=0, has_side_effects=True, vmem_limit_bytes=60 * 1024 * 1024
        ),
    )(hidden, query, keys, values, attends, levels, weight, gate_table)


def shards(hidden, query, keys, values, attends, levels, out_weight, gate_table):
    weight = out_weight.reshape(HEADS, HS, D)
    return fused(hidden, query, keys, values, attends, levels, weight, gate_table)


def solution(mesh):
    fine = Mesh(mesh.devices.reshape(NZ, NX, NC, NY), ("z", "x", "c", "head"))
    tokens = P(("z", "x", "c", "head"), None)
    group = ("z", "x", "c")
    placed = (
        tokens, tokens, tokens, tokens, P(group, None), P(group), P("head", None), P(),
    )
    return jax.shard_map(
        shards, mesh=fine, in_specs=placed, out_specs=tokens, check_vma=False
    )
```

time: 938 us -> 71.6 us (0.08)
  waiting for transfers between devices: 471 us -> 0 us
  starting transfers between devices: 254 us -> 0 us
  local copies, waits for them, and re-layouts: 88.6 us -> 1.77 us
  Pallas kernels: 0 us -> 67.8 us
  matrix products: 50.4 us -> 0 us
  loops' own time: 40 us -> 0 us
  between operations: 14.2 us -> 0.66 us
  other arithmetic: 12.8 us -> 0 us
    ppermute x126 -> x0, waiting for transfers between devices: 357 us -> none  [from_behind(): return lax.ppermute(block, axis, route)]
    ppermute x126 -> x0, starting transfers between devices: 243 us -> none  [from_behind(): return lax.ppermute(block, axis, route)]
    reduce_scatter x1 -> x0, waiting for transfers between devices: 99.1 us -> none  [shards(): lax.psum_scatter(jnp.dot(attended, out_weight, preferred_element_type=jnp...]
    pallas_call x0 -> x1, Pallas kernels: none -> 67.8 us  [fused(): pl.pallas_call(kernel, out_shape=jax.ShapeDtypeStruct((PART, D), BF16), i...]
    dot_general x129 -> x0, matrix products: 50.4 us -> none  [the longest x64 27.6 us: absorb(): jnp.einsum('hqk,khd->hqd', weights.astype(jnp.bfloat16), value_three, pre...]
    while x192 -> x0, local copies, waits for them, and re-layouts: 45 us -> none
    another operation x1 -> x0, loops' own time: 40 us -> none  [shards(): lax.fori_loop(1, lax.axis_size('group'), chain_step, ((local_keys, local_...]
    dynamic_slice x64 -> x0, local copies, waits for them, and re-layouts: 37.4 us -> none  [the longest x63 36.5 us: chain_step(): lax.dynamic_index_in_dim(attend_row, clipped, 0, keepdims=False) > 0]
  transfers between devices with their start and end apart: 130 -> 0, of which waited for: 130 -> 0; matrix products, arithmetic and copies ran while one was open for 8% -> 0% of each run, Pallas kernels for 0% -> 0%
where the time goes in v3:
time: 71.6 us; the launch traced here: 70.2 us
  Pallas kernels  67.8 us (95%)
  local copies, waits for them, and re-layouts  1.77 us (2%)
    pallas_call x1, Pallas kernels, fused(): pl.pallas_call(kernel, out_shape=jax.ShapeDtypeStruct((PART, D), BF16), i...  67.8 us
    unnamed x1, local copies, waits for them, and re-layouts  1.77 us

profile of v3, /device:TPU:224, one launch (start us, length us, event | category | flops | bytes accessed | tf_op | source)
XLA Modules:
  0.0 70.2 jit_solution(2677012128845665781)
XLA Ops:
  0.7 67.8 %shard_map.82 = bf16[64,3072]{1,0:T(8,128)(2,1)} custom-call(bf16[64,3072]{1,0:T(8,128)(2,1)} %hidden_hbm.1, bf16[64,1536]{1,0:T(8,128)(2,1)} %q_hbm.1, bf16[64,1536]{1,0:T(8,128)(2,1)} %k_hbm.1, bf16[64,1536]{1,0:T(8,128)(2,1)} %v_hbm.1, s32[1,64]{1,0:T(1,128)} %attends_hbm.1, s32[1]{0:T(128)S(6)} %copy.10.level_ref, bf16[3,128,3072]{2,1,0:T(8,128)(2,1)} %bitcast.1, ...), custom_call_target="tpu_custom_call" | custom-call | tf_op jit(solution)/shard_map/pallas_call | solution.py:401
  68.5 1.8 %copy.11 = bf16[64,3072]{1,0:T(8,128)(2,1)} copy(bf16[64,3072]{1,0:T(8,128)(2,1)} %shard_map.82) | data formatting | bytes 786432

commit v4 on v3

--- a/solution.py
+++ b/solution.py
@@ -19,6 +19,10 @@
 LAST = 4
 SCALE = 1.4426950408889634 * HS**-0.5
 NONE = -1e30
+ORDER = tuple((s, h) for s in range(3) for h in range(3)) + (
+    (3, 0), (3, 1), (4, 0), (3, 2), (4, 2), (4, 1),
+)
+TAKEN = (3, 4, 5, 5, 6, 7, 8, 8, 9, 10, 11, 12, 13, 14, 14)
 MESH_ID = pl.DeviceIdType.MESH
 F32, BF16 = jnp.float32, jnp.bfloat16
 
@@ -30,7 +34,8 @@
     early_sem, token_send, kv_sem, q_sem, bias_send, bias_recv, q_send, q_recv,
     up_send, dn_send, z_recv, sib_send, sib_recv,
     o_send, o_recv, s_send, s_recv, y_send, y_recv,
-    w_send, w_recv, far_send, far_recv, near_send, near_recv, side_send, side_recv, out_sem,
+    w_send, w_recv, far_send, far_recv, swap_send, swap_recv, swap_far_send, swap_far_recv,
+    near_send, near_recv, side_send, side_recv, out_sem,
 ):
     z, x, c, y = (lax.axis_index(a) for a in ("z", "x", "c", "head"))
     above, below = (z + 1) % NZ, (z + NZ - 1) % NZ
@@ -80,13 +85,16 @@
             token_send.at[a], landed(a, h), dy=dest,
         )
 
-    for h in range(HEADS):
+    def token_start(h):
         for a in range(3):
             for d in (2, 1, 3):
                 token_copy(a, h, d).start()
             pltpu.make_async_copy(
                 sources[a].at[:, span(y * HEADS + h, HS)], landing(a, h), landed(a, h)
             ).start()
+
+    token_start(0)
+    token_start(1)
 
     def up_copy(b, h):
         ref = kv.at[b, h, c]
@@ -145,46 +153,81 @@
 
     ahead, behind, opposite = (y + 1) % NY, (y + NY - 1) % NY, (y + 2) % NY
 
-    def weight_ref(h, owner, part):
-        rows = span(owner, HS) if part is None else span(owner * 2 + part, HS // 2)
+    odd = x % 2
+    partner = ((x + 1 - 2 * odd) % NX, (x + NX - 1 + 2 * odd) % NX)
+
+    def weight_ref(h, owner, part, parts):
+        size = HS // parts
+        rows = pl.ds(pl.multiple_of(owner * HS + part * size, size), size)
         return wbuf.at[h, rows, span(c, HALF)]
 
     def weight_bytes(h, rows):
         return wbuf.at[h, 0:rows, 0:HALF]
 
+    def shared(h):
+        return h < 1
+
+    def fetched(h, owner):
+        return weight_ref(h, owner, odd, 2) if shared(h) else weight_ref(h, owner, 0, 1)
+
     def weight_copy(h, way):
+        source = w_hbm.at[h, :, span(c, HALF)]
+        if shared(h):
+            source = w_hbm.at[h, span(odd, HS // 2), span(c, HALF)]
         return remote(
-            w_hbm.at[h, :, span(c, HALF)], weight_ref(h, y, None),
-            w_send.at[h], w_recv.at[h], dy=(ahead, behind)[way],
+            source, fetched(h, y), w_send.at[h], w_recv.at[h], dy=(ahead, behind)[way]
         )
 
     def far_copy(h, way):
-        ref = weight_ref(h, (behind, ahead)[way], way)
+        part, parts = (odd * 2 + way, 4) if shared(h) else (way, 2)
+        ref = weight_ref(h, (behind, ahead)[way], part, parts)
         return remote(ref, ref, far_send.at[h], far_recv.at[h], dy=(ahead, behind)[way])
 
+    def swap_copy(h, owner, send, recv):
+        ref = fetched(h, owner)
+        return remote(ref, ref, send.at[h], recv.at[h], dx=partner[h])
+
     def near_side(h, way):
-        ref = weight_ref(h, (behind, ahead)[way], None)
+        ref = weight_ref(h, (behind, ahead)[way], 0, 1)
         return remote(ref, ref, near_send.at[h], near_recv.at[h], dc=1 - c)
 
-    def far_side(h, way):
-        ref = weight_ref(h, opposite, way)
+    def far_side(h):
+        ref = weight_ref(h, opposite, 0, 1)
         return remote(ref, ref, side_send.at[h], side_recv.at[h], dc=1 - c)
+
+    def near_rows(h):
+        return HS if shared(h) else 2 * HS
 
     def weight_start(h):
         for way in range(2):
             weight_copy(h, way).start()
 
     def weight_near(h):
-        wait_bytes(weight_bytes(h, 2 * HS), w_recv.at[h])
+        wait_bytes(weight_bytes(h, near_rows(h)), w_recv.at[h])
         for way in range(2):
             far_copy(h, way).start()
+        if shared(h):
+            for owner in (behind, ahead):
+                swap_copy(h, owner, swap_send, swap_recv).start()
+        else:
+            for way in range(2):
+                near_side(h, way).start()
+
+    def weight_near_swapped(h):
+        wait_bytes(weight_bytes(h, HS), swap_recv.at[h])
         for way in range(2):
             near_side(h, way).start()
 
     def weight_far(h):
-        wait_bytes(weight_bytes(h, HS), far_recv.at[h])
-        for way in range(2):
-            far_side(h, way).start()
+        wait_bytes(weight_bytes(h, near_rows(h) // 2), far_recv.at[h])
+        if shared(h):
+            swap_copy(h, opposite, swap_far_send, swap_far_recv).start()
+        else:
+            far_side(h).start()
+
+    def weight_far_swapped(h):
+        wait_bytes(weight_bytes(h, HS // 2), swap_far_recv.at[h])
+        far_side(h).start()
 
     for h in range(HEADS):
         wait_bytes(kvin.at[h], kv_sem.at[h])
@@ -193,6 +236,8 @@
         kv[z, h, c, ROWS : ROWS + HS, :] = turned[:, :HS]
         kv[z, h, c, ROWS + HS :, :] = turned[:, HS:]
         each_move(z, h, own_plan(h), start)
+        if h == 0:
+            token_start(2)
         wait_bytes(qin.at[h], q_sem.at[h])
         qt[h, x] = qin[h].T
         for d in (2, 1, 3):
@@ -322,35 +367,56 @@
                 _, b, moves = plan(step, h)
                 each_move(b, h, moves, ended)
 
-    @pl.loop(0, (LAST + 1) * HEADS + 1)
+    def pick(i, entries):
+        value = jnp.int32(entries[0])
+        for at in range(1, len(entries)):
+            if entries[at] != entries[at - 1]:
+                value = jnp.where(i >= at, entries[at], value)
+        return value
+
+    steps, heads = [s for s, _ in ORDER], [h for _, h in ORDER]
+    first = [HEADS] + [t + 1 for t in TAKEN[:-1]]
+    weight_plan = {
+        4: lambda: weight_near(0),
+        6: lambda: weight_near(1),
+        8: lambda: weight_near_swapped(0),
+        9: lambda: weight_near(2),
+        11: lambda: (weight_far(0), weight_far(1)),
+    }
+
+    @pl.loop(0, len(ORDER))
     def _(i):
-        step, h = i // HEADS, i % HEADS
-
-        when(step < LAST - 1, lambda: arrive(step + 1, h))
-        when(step == LAST, lambda: arrive(step, h))
+        step, h = pick(i, steps), pick(i, heads)
+
+        @pl.loop(pick(i, first), pick(i, TAKEN) + 1)
+        def _(j):
+            arrive(pick(j, steps), pick(j, heads))
+
         when(step == 0, lambda: wait_bytes(qt.at[h, 0 : NX - 1], q_recv.at[h]))
         when(i == 0, lambda: wait_bytes(bias.at[0 : NX - 1], bias_recv))
 
         low = jnp.maximum(z - step, 0)
         high = (z + step) % NZ
-        has_low = (step <= LAST) & (z >= step) & reaches_up(low, h, z)
-        has_high = (step > 0) & (step <= LAST) & reaches_down(high, h, z) & (high < z)
+        has_low = (z >= step) & reaches_up(low, h, z)
+        has_high = (step > 0) & reaches_down(high, h, z) & (high < z)
         when(has_low, lambda: side_copy(low, h, 1 - c).wait_recv())
         when(has_high, lambda: side_copy(high, h, 1 - c).wait_recv())
         when(has_low & has_high, lambda: attend([low, high], h))
         when(has_low != has_high, lambda: attend([jnp.where(has_low, low, high)], h))
 
-        for at, piece in ((4, 0), (7, 1), (11, 2)):
-            when(i == at, lambda piece=piece: weight_near(piece))
-
         @pl.when(step == LAST)
         def _():
             hand_over(h)
             settle(h)
 
-        when(i > LAST * HEADS, lambda: merge((i - 1) % HEADS))
-
-    weight_far(0)
+        for at, act in weight_plan.items():
+            when(i == at, act)
+        when(i == len(ORDER) - 2, lambda: merge(0))
+
+    weight_far_swapped(0)
+    weight_far(2)
+    merge(2)
+    merge(1)
     for a in range(3):
         wait_bytes(sources[a].at[:, 0 : 3 * HEADS * HS], token_send.at[a])
     wait_bytes(bias.at[0 : NX - 1], bias_send)
@@ -363,8 +429,17 @@
         return pltpu.make_async_copy(out.at[:, columns], out_hbm.at[:, columns], out_sem.at[j])
 
     for h in range(HEADS):
-        if h > 0:
-            weight_far(h)
+        wait_bytes(osend.at[h], o_send.at[h])
+        wait_bytes(ssend.at[h], s_send.at[h])
+        wait_bytes(att.at[h, 0 : 3 * PART], y_send.at[h])
+        wait_bytes(weight_bytes(h, near_rows(h)), w_send.at[h])
+        wait_bytes(weight_bytes(h, near_rows(h) // 2), far_send.at[h])
+        if shared(h):
+            wait_bytes(weight_bytes(h, HS), swap_send.at[h])
+            wait_bytes(weight_bytes(h, HS // 2), swap_far_send.at[h])
+        wait_bytes(weight_bytes(h, 2 * HS), near_send.at[h])
+        wait_bytes(weight_bytes(h, HS), side_send.at[h])
+    for h in (0, 2, 1):
         wait_bytes(weight_bytes(h, 2 * HS), near_recv.at[h])
         wait_bytes(arecv.at[h], y_recv.at[h])
         wait_bytes(weight_bytes(h, HS), side_recv.at[h])
@@ -373,21 +448,13 @@
             part = jnp.dot(arecv[h], wbuf[h, :, columns], preferred_element_type=F32)
             if h > 0:
                 part = part + summed[:, columns]
-            if h < HEADS - 1:
+            if h != 1:
                 summed[:, columns] = part
             else:
                 gated = gates[pl.ds(level_ref[0], 1), columns] * part
                 out[:, columns] = (hidden[:, columns].astype(F32) + gated).astype(BF16)
                 out_copy(j).start()
 
-    for h in range(HEADS):
-        wait_bytes(osend.at[h], o_send.at[h])
-        wait_bytes(ssend.at[h], s_send.at[h])
-        wait_bytes(att.at[h, 0 : 3 * PART], y_send.at[h])
-        wait_bytes(weight_bytes(h, 2 * HS), w_send.at[h])
-        wait_bytes(weight_bytes(h, HS), far_send.at[h])
-        wait_bytes(weight_bytes(h, 2 * HS), near_send.at[h])
-        wait_bytes(weight_bytes(h, HS), side_send.at[h])
     for j in range(D // TILE):
         out_copy(j).wait()
 
@@ -428,7 +495,8 @@
             dma((4,)), dma((3,)), each, each, dma(()), dma(()), each, each,
             moving, moving, moving, moving, moving,
             each, each, each, each, each, each,
-            each, each, each, each, each, each, each, each, dma((D // TILE,)),
+            each, each, each, each, each, each, each, each,
+            each, each, each, each, dma((D // TILE,)),
         ],
         compiler_params=pltpu.CompilerParams(
             collective_id=0, has_side_effects=True, vmem_limit_bytes=60 * 1024 * 1024

time: 71.6 us -> 66.6 us (0.930); the launches traced: 70.2 us -> 66.4 us
  Pallas kernels: 67.8 us -> 64 us
    pallas_call x1, Pallas kernels: 67.8 us -> 64 us  [fused(): pl.pallas_call(kernel, out_shape=jax.ShapeDtypeStruct((PART, D), BF16), i...]
where the time goes in v4:
time: 66.6 us; the launch traced here: 66.4 us
  Pallas kernels  64 us (96%)
  local copies, waits for them, and re-layouts  1.77 us (3%)
    pallas_call x1, Pallas kernels, fused(): pl.pallas_call(kernel, out_shape=jax.ShapeDtypeStruct((PART, D), BF16), i...  64 us
    unnamed x1, local copies, waits for them, and re-layouts  1.77 us

profile of v4, /device:TPU:224, one launch (start us, length us, event | category | flops | bytes accessed | tf_op | source)
XLA Modules:
  0.0 66.4 jit_solution(11517934192375883227)
XLA Ops:
  0.7 64.0 %shard_map.82 = bf16[64,3072]{1,0:T(8,128)(2,1)} custom-call(bf16[64,3072]{1,0:T(8,128)(2,1)} %hidden_hbm.1, bf16[64,1536]{1,0:T(8,128)(2,1)} %q_hbm.1, bf16[64,1536]{1,0:T(8,128)(2,1)} %k_hbm.1, bf16[64,1536]{1,0:T(8,128)(2,1)} %v_hbm.1, s32[1,64]{1,0:T(1,128)} %attends_hbm.1, s32[1]{0:T(128)S(6)} %copy.10.level_ref, bf16[3,128,3072]{2,1,0:T(8,128)(2,1)} %bitcast.1, ...), custom_call_target="tpu_custom_call" | custom-call | tf_op jit(solution)/shard_map/pallas_call | solution.py:468
  64.7 1.8 %copy.11 = bf16[64,3072]{1,0:T(8,128)(2,1)} copy(bf16[64,3072]{1,0:T(8,128)(2,1)} %shard_map.82) | data formatting | bytes 786432

commit v5 on v4

--- a/solution.py
+++ b/solution.py
@@ -85,16 +85,15 @@
             token_send.at[a], landed(a, h), dy=dest,
         )
 
-    def token_start(h):
-        for a in range(3):
-            for d in (2, 1, 3):
-                token_copy(a, h, d).start()
-            pltpu.make_async_copy(
-                sources[a].at[:, span(y * HEADS + h, HS)], landing(a, h), landed(a, h)
-            ).start()
-
-    token_start(0)
-    token_start(1)
+    def token_start(a, h):
+        for d in (2, 1, 3):
+            token_copy(a, h, d).start()
+        pltpu.make_async_copy(
+            sources[a].at[:, span(y * HEADS + h, HS)], landing(a, h), landed(a, h)
+        ).start()
+
+    for a, h in ((0, 0), (1, 0), (2, 0), (2, 1), (0, 1), (1, 1), (2, 2), (0, 2), (1, 2)):
+        token_start(a, h)
 
     def up_copy(b, h):
         ref = kv.at[b, h, c]
@@ -229,19 +228,27 @@
         wait_bytes(weight_bytes(h, HS // 2), swap_far_recv.at[h])
         far_side(h).start()
 
-    for h in range(HEADS):
+    def own_block(h):
         wait_bytes(kvin.at[h], kv_sem.at[h])
         kv[z, h, c, 0:ROWS, :] = kvin[h, 0]
         turned = kvin[h, 1].T
         kv[z, h, c, ROWS : ROWS + HS, :] = turned[:, :HS]
         kv[z, h, c, ROWS + HS :, :] = turned[:, HS:]
         each_move(z, h, own_plan(h), start)
-        if h == 0:
-            token_start(2)
+
+    def own_query(h):
         wait_bytes(qin.at[h], q_sem.at[h])
         qt[h, x] = qin[h].T
         for d in (2, 1, 3):
             query_copy(h, d).start()
+
+    own_block(0)
+    own_query(0)
+    own_query(1)
+    own_block(1)
+    own_query(2)
+    own_block(2)
+    for h in range(HEADS):
         weight_start(h)
 
     attends_copy.wait()
@@ -407,7 +414,6 @@
         @pl.when(step == LAST)
         def _():
             hand_over(h)
-            settle(h)
 
         for at, act in weight_plan.items():
             when(i == at, act)
@@ -428,6 +434,8 @@
         columns = pl.ds(j * TILE, TILE)
         return pltpu.make_async_copy(out.at[:, columns], out_hbm.at[:, columns], out_sem.at[j])
 
+    for h in range(HEADS):
+        settle(h)
     for h in range(HEADS):
         wait_bytes(osend.at[h], o_send.at[h])
         wait_bytes(ssend.at[h], s_send.at[h])

time: 66.6 us -> 66.5 us (level)
  no operation moved by 1% of the time
where the time goes in v5:
time: 66.5 us; the launch traced here: 66.4 us
  Pallas kernels  63.9 us (96%)
  local copies, waits for them, and re-layouts  1.77 us (3%)
    pallas_call x1, Pallas kernels, fused(): pl.pallas_call(kernel, out_shape=jax.ShapeDtypeStruct((PART, D), BF16), i...  63.9 us
    unnamed x1, local copies, waits for them, and re-layouts  1.77 us

profile of v5, /device:TPU:224, one launch (start us, length us, event | category | flops | bytes accessed | tf_op | source)
XLA Modules:
  0.0 66.4 jit_solution(6554145069348999946)
XLA Ops:
  0.7 63.9 %shard_map.82 = bf16[64,3072]{1,0:T(8,128)(2,1)} custom-call(bf16[64,3072]{1,0:T(8,128)(2,1)} %hidden_hbm.1, bf16[64,1536]{1,0:T(8,128)(2,1)} %q_hbm.1, bf16[64,1536]{1,0:T(8,128)(2,1)} %k_hbm.1, bf16[64,1536]{1,0:T(8,128)(2,1)} %v_hbm.1, s32[1,64]{1,0:T(1,128)} %attends_hbm.1, s32[1]{0:T(128)S(6)} %copy.10.level_ref, bf16[3,128,3072]{2,1,0:T(8,128)(2,1)} %bitcast.1, ...), custom_call_target="tpu_custom_call" | custom-call | tf_op jit(solution)/shard_map/pallas_call | solution.py:476
  64.6 1.8 %copy.11 = bf16[64,3072]{1,0:T(8,128)(2,1)} copy(bf16[64,3072]{1,0:T(8,128)(2,1)} %shard_map.82) | data formatting | bytes 786432
